TPU v7x, 32 devices: a whole 2x2x4 slice. The times are simulated.
32 devices in a mesh: seq: 8 (over z, core), chan: 4 (over y, x).
Axes of the slice: x: 2, y: 2, z: 4, core: 2. Of those that a mesh axis runs over, the one named last changes fastest.
Arguments:
- mixer_input: bfloat16 [1024, 2048], P('seq', 'chan'), may hold values from -6 to 6
- gate_branch: bfloat16 [1024, 2048], P('seq', 'chan'), may hold values from -6 to 6
- skip_gain: float32 [2048], P('chan'), may hold values from -3 to 3
- decay_rate: float32 [2048], P('chan'), may hold values from 0.1 to 64
- first_weight: float32 [33, 64], replicated, may hold values from -1 to 1
- first_bias: float32 [64], replicated, may hold values from -4 to 4
- second_weight: float32 [64, 64], replicated, may hold values from -0.75 to 0.75
- second_bias: float32 [64], replicated, may hold values from -4 to 4
- last_weight: float32 [64, 2048], P(None, 'chan'), may hold values from -0.75 to 0.75
- output_weight: bfloat16 [2048, 4096], P('chan'), may hold values from -0.1875 to 0.1875
Outputs:
- projected: bfloat16 [1024, 4096], P('seq', 'chan')
All inputs are finite; a program needn't handle non-finite values.
Results may differ from a plain program's by a relative error of at most 0.0049.
Values may be sent and summed in bfloat16 or wider, within the bound.
No kernel may reach another device: no remote copies, remote signals or barrier semaphores. Data moves between devices by JAX's collectives and lax.ppermute only.
A program may use at most 64 MiB of HBM per device.

v0:
```python
import functools
import math

import jax
import jax.numpy as jnp
import numpy as np
from jax import lax
from jax.experimental import pallas as pl
from jax.experimental.pallas import tpu as pltpu
from jax.sharding import PartitionSpec as P

HIGHEST = lax.Precision.HIGHEST
F32 = jnp.float32
BF16 = jnp.bfloat16
LANES = 128
FACE = 4
VMEM = pltpu.VMEM


def feature_table(length, emb_width):
    band_count = (emb_width - 1) // 2
    positions = np.arange(length, dtype=np.int64)
    columns = [positions / length]
    for band in range(1, band_count + 1):
        frequency = min(
            length // 2, max(band, int((length / 2) ** ((band - 1) / (band_count - 1))))
        )
        angle = (positions * frequency % length) * (2.0 * math.pi / length)
        columns.append(np.cos(angle))
        columns.append(np.sin(angle))
    return np.stack(columns, axis=1).astype(np.float32)


def split_bf16(table):
    high = table.astype(np.float32).astype(jnp.bfloat16)
    low = (table - high.astype(np.float64)).astype(np.float32).astype(jnp.bfloat16)
    return high, low


def dft_tables(block):
    size = 2 * block
    bins = np.arange(block)[:, None]
    times = np.arange(block)[None, :]
    angle = (bins * times % size) * (2.0 * math.pi / size)
    imag = -np.sin(angle)
    imag[0] = 1.0 - 2.0 * (np.arange(block) % 2)
    forward = np.concatenate([np.cos(angle), imag], axis=0)
    weight = np.where(bins == 0, 1.0, 2.0) / size
    back_imag = -weight * np.sin(angle)
    back_imag[0] = (1.0 - 2.0 * (np.arange(block) % 2)) / size
    inverse = np.concatenate([weight * np.cos(angle), back_imag], axis=0).T
    return forward, inverse


def fast_sin(x):
    turns = jnp.floor(x * (1.0 / math.pi) + 0.5)
    rest = x - turns * 3.140625
    rest = rest - turns * 9.67502593994140625e-4
    rest = rest - turns * 1.509957990978376432e-7
    parity = turns - 2.0 * jnp.floor(turns * 0.5)
    rest = rest * (1.0 - 2.0 * parity)
    square = rest * rest
    poly = -2.5052108e-8
    for coeff in (2.7557319e-6, -1.9841270e-4, 8.3333333e-3, -1.6666667e-1):
        poly = poly * square + coeff
    return rest + rest * square * poly


def expm1_of_negative(x):
    near = jnp.maximum(x, -0.5)
    series = jnp.full_like(x, 1.0 / 3628800.0)
    for denom in (362880.0, 40320.0, 5040.0, 720.0, 120.0, 24.0, 6.0, 2.0, 1.0):
        series = series * near + 1.0 / denom
    return jnp.where(x > -0.5, near * series, jnp.exp(x) - 1.0)


def split_value(value):
    high = value.astype(BF16)
    return high, (value - high.astype(F32)).astype(BF16)


def filter_feature_table(length, emb_width, pad):
    table = feature_table(length, emb_width)
    columns = []
    for half in (table[: length // 2], table[length // 2 :]):
        high, low = (part.astype(np.float32) for part in split_bf16(half))
        for part in (high, high, low):
            columns.append(np.pad(part, ((0, 0), (0, pad - emb_width))))
    return np.concatenate(columns, axis=1)


def twice_diagonal(value):
    zero = jnp.zeros_like(value)
    return jnp.concatenate(
        [jnp.concatenate([value, zero], axis=1), jnp.concatenate([zero, value], axis=1)], axis=0
    )


def stacked_diagonal(value):
    high, low = split_value(value)
    high = twice_diagonal(high.astype(F32))
    low = twice_diagonal(low.astype(F32))
    return jnp.concatenate([high, low, high], axis=0).astype(BF16)


def layer(value, weight):
    high, low = split_value(value)
    return jnp.dot(
        jnp.concatenate([high, high, low], axis=1), weight, preferred_element_type=F32
    )


def filter_kernel(blocks, block, outs, pad, *refs):
    hbm, refs = refs[:10], refs[10:]
    hre_ref, him_ref, hfirst_ref, fwd_ref, inv_ref, skip_ref = refs[:6]
    refs = refs[6:]
    w1_ref, b1_ref, w2_ref, b2_ref, w3_ref, decay_ref, feat_ref, table_ref, back_ref = refs[:9]
    all_skip_ref, first_ref, sems = refs[9:]
    targets = [
        w1_ref, feat_ref, b1_ref, w2_ref, b2_ref, w3_ref, decay_ref, table_ref, back_ref,
        all_skip_ref,
    ]
    copies = [
        pltpu.make_async_copy(hbm[i], targets[i], sems.at[i]) for i in range(len(targets))
    ]
    for copy in copies:
        copy.start()
    group = lax.axis_index("seq") % outs
    length = blocks * block
    emb, order = w1_ref.shape
    first_ref[...] = jnp.zeros_like(first_ref)
    for copy in copies[:7]:
        copy.wait()

    high, low = split_value(w1_ref[...])
    high, low = high.astype(F32), low.astype(F32)
    zero = jnp.zeros_like(high)
    for i, part in enumerate((high, low, high)):
        first_ref[i * pad : i * pad + emb] = jnp.concatenate([part, zero], axis=1)
        first_ref[(3 + i) * pad : (3 + i) * pad + emb] = jnp.concatenate([zero, part], axis=1)
    b1 = jnp.concatenate([b1_ref[...]] * 2, axis=1)
    b2 = jnp.concatenate([b2_ref[...]] * 2, axis=1)
    hidden = fast_sin(
        jnp.dot(
            feat_ref[...].astype(BF16), first_ref[...].astype(BF16), preferred_element_type=F32
        )
        + b1
    )
    hidden = fast_sin(layer(hidden, stacked_diagonal(w2_ref[...])) + b2)
    lanes = pl.ds(pl.multiple_of(group * LANES, LANES), LANES)
    shaped = layer(hidden, stacked_diagonal(w3_ref[:, lanes]))

    decay = decay_ref[:, lanes]
    energy = expm1_of_negative(-2.0 * decay) / expm1_of_negative(decay * (-2.0 / length))
    times = lax.broadcasted_iota(jnp.int32, (length // 2, LANES), 0).astype(F32) * (1.0 / length)
    window = jnp.exp(-(decay * times)) * (1.0 / jnp.sqrt(energy))
    window = jnp.concatenate([window, window * jnp.exp(-0.5 * decay)], axis=1)
    taps_high, taps_low = split_value(shaped * window)

    copies[7].wait()
    high, low = split_value(table_ref[...])
    fwd_ref[:, :block] = high
    fwd_ref[:, block:] = low
    table = jnp.concatenate([high, low, high], axis=1)
    rows = lax.broadcasted_iota(jnp.int32, (2 * block, LANES), 0)
    sign = (1 - 2 * lax.rem(rows, 2)).astype(F32)
    first_row = lax.broadcasted_iota(jnp.int32, (block, LANES), 0) == 0
    spectra = [None] * blocks
    for k in range(blocks // 2):
        part = slice(k * block, (k + 1) * block)
        stacked = jnp.concatenate([taps_high[part], taps_high[part], taps_low[part]], axis=0)
        now = jnp.dot(table, stacked, preferred_element_type=F32)
        spectra[k], spectra[k + blocks // 2] = now[:, :LANES], now[:, LANES:]
    for k in range(blocks):
        spec = spectra[k] if k == 0 else spectra[k] + sign * spectra[k - 1]
        real, imag = spec[:block], spec[block:]
        hre_ref[k] = real
        him_ref[k] = jnp.where(first_row, 0.0, imag)
        hfirst_ref[k] = jnp.where(first_row, imag, real)[:8]

    copies[8].wait()
    copies[9].wait()
    skip_ref[...] = all_skip_ref[:, lanes]
    high, low = split_value(back_ref[...])
    inv_ref[:, : 2 * block] = high
    inv_ref[:, 2 * block : 4 * block] = low
    inv_ref[:, 4 * block :] = high


def call_filter(weights, skip, blocks, outs, block):
    w1, b1, w2, b2, w3, decay = weights
    length = blocks * block
    emb, order = w1.shape
    pad = -(-emb // 8) * 8
    forward, inverse = dft_tables(block)
    feats = filter_feature_table(length, emb, pad)
    hbm = [
        w1, feats, b1[None], w2, b2[None], w3, decay[None], forward.astype(np.float32),
        inverse.astype(np.float32), skip[None],
    ]
    out_shape = [
        VMEM((blocks, block, LANES), F32),
        VMEM((blocks, block, LANES), F32),
        VMEM((blocks, 8, LANES), F32),
        VMEM((2 * block, 2 * block), BF16),
        VMEM((block, 6 * block), BF16),
        VMEM((1, LANES), F32),
    ]
    return pl.pallas_call(
        functools.partial(filter_kernel, blocks, block, outs, pad),
        in_specs=[pl.BlockSpec(memory_space=pltpu.HBM)] * len(hbm),
        out_specs=[pl.BlockSpec(memory_space=VMEM)] * len(out_shape),
        out_shape=out_shape,
        scratch_shapes=[
            VMEM(w1.shape, F32),
            VMEM((1, order), F32),
            VMEM(w2.shape, F32),
            VMEM((1, order), F32),
            VMEM(w3.shape, F32),
            VMEM((1, w3.shape[1]), F32),
            VMEM(feats.shape, F32),
            VMEM(forward.shape, F32),
            VMEM(inverse.shape, F32),
            VMEM((1, skip.shape[0]), F32),
            VMEM((6 * pad, 2 * order), F32),
            pltpu.SemaphoreType.DMA((len(hbm),)),
        ],
        compiler_params=pltpu.CompilerParams(vmem_limit_bytes=32 * 2**20),
        cost_estimate=pl.CostEstimate(
            flops=4 * 10**8, bytes_accessed=8 * 2**20, transcendentals=length * LANES
        ),
        name="filter_spectra",
    )(*(pltpu.with_memory_space_constraint(jnp.asarray(each), pltpu.HBM) for each in hbm))


def columns_of(part, half, width):
    return pl.ds(pl.multiple_of(part * width + half * (width // 2), LANES), width // 2)


def weight_copies(weight_ref, over_x_ref, over_y_ref, sems, first_sem):
    rows = weight_ref.shape[0] // 2
    width = weight_ref.shape[1] // FACE
    me = lax.axis_index("chan")
    half_rows = pl.ds(pl.multiple_of((lax.axis_index("seq") % 2) * rows, LANES), rows)
    copies = []
    for out_ref, half, parts in ((over_x_ref, 0, (1, 3)), (over_y_ref, 1, (2, 3))):
        for place, k in enumerate(parts):
            copies.append(
                pltpu.make_async_copy(
                    weight_ref.at[half_rows, columns_of(me ^ k, half, width)],
                    out_ref.at[:, place * (width // 2) : (place + 1) * (width // 2)],
                    sems.at[first_sem + len(copies)],
                )
            )
    return copies


def pack_kernel(blocks, outs, x_ref, gate_ref, weight_ref, pieces_ref, *refs):
    gate_refs, (over_x_ref, over_y_ref, sems) = refs[:outs], refs[outs:]
    group = lax.axis_index("seq") % outs
    copies = [
        pltpu.make_async_copy(
            x_ref.at[:, (d % outs) * LANES : (d % outs + 1) * LANES], pieces_ref.at[d], sems.at[d]
        )
        for d in range(blocks)
    ]
    for k in range(outs):
        lanes = pl.ds(pl.multiple_of((group ^ k) * LANES, LANES), LANES)
        copies.append(
            pltpu.make_async_copy(gate_ref.at[:, lanes], gate_refs[k], sems.at[len(copies)])
        )
    copies += weight_copies(weight_ref, over_x_ref, over_y_ref, sems, len(copies))
    for copy in copies:
        copy.start()
    for copy in copies:
        copy.wait()


def call_pack(x, gate, weight, blocks, outs):
    block = x.shape[0]
    send = VMEM((weight.shape[0] // 2, weight.shape[1] // FACE), BF16)
    out_shape = [jax.ShapeDtypeStruct((blocks, block, LANES), BF16)]
    out_shape += [jax.ShapeDtypeStruct((block, LANES), BF16)] * outs + [send] * 2
    return pl.pallas_call(
        functools.partial(pack_kernel, blocks, outs),
        in_specs=[pl.BlockSpec(memory_space=pltpu.HBM)] * 3,
        out_specs=[pl.BlockSpec(memory_space=VMEM)] * len(out_shape),
        out_shape=out_shape,
        scratch_shapes=[pltpu.SemaphoreType.DMA((blocks + outs + 4,))],
        cost_estimate=pl.CostEstimate(flops=0, bytes_accessed=2**21, transcendentals=0),
        name="pack_pieces",
    )(*(pltpu.with_memory_space_constraint(each, pltpu.HBM) for each in (x, gate, weight)))


def conv_kernel(blocks, outs, block, xs_ref, *refs):
    gate_refs, refs = refs[:outs], refs[outs:]
    hre_ref, him_ref, hfirst_ref, fwd_ref, inv_ref, skip_ref = refs[:6]
    refs = refs[8:]
    out_refs, (wre_ref, wim_ref, yre_ref, yim_ref) = refs[:outs], refs[outs + 2 :]
    me = lax.axis_index("seq")
    half, group = me // outs, me % outs
    earlier = blocks - outs
    for j in range(outs):
        values = jnp.concatenate([xs_ref[j], xs_ref[half * outs + j]], axis=1)
        spec = jnp.dot(
            fwd_ref[...], jnp.concatenate([values, values], axis=0), preferred_element_type=F32
        )
        before = jnp.where(half > 0, spec[:, :LANES], 0.0)
        wre_ref[j] = before[:block]
        wim_ref[j] = before[block:]
        wre_ref[earlier + j] = spec[:block, LANES:]
        wim_ref[earlier + j] = spec[block:, LANES:]

    def rows_at(start, first):
        rows = pl.ds(start, 8)
        wre = [wre_ref[j, rows, :] for j in range(blocks)]
        wim = [wim_ref[j, rows, :] for j in range(blocks)]
        for o in range(outs):
            total_re = total_im = None
            for j in range(earlier + o + 1):
                k = earlier + o - j
                hre = hre_ref[k, rows, :]
                him = him_ref[k, rows, :]
                hother = hfirst_ref[k] if first else hre
                add_re = wre[j] * hre - wim[j] * him
                add_im = wre[j] * him + wim[j] * hother
                total_re = add_re if total_re is None else total_re + add_re
                total_im = add_im if total_im is None else total_im + add_im
            yre_ref[o, rows, :] = total_re
            yim_ref[o, rows, :] = total_im

    rows_at(0, True)

    @pl.loop(1, block // 8)
    def _(tile):
        rows_at(pl.multiple_of(tile * 8, 8), False)

    def stacked(slot):
        re_high, re_low = split_value(yre_ref[slot])
        im_high, im_low = split_value(yim_ref[slot])
        return jnp.concatenate([re_high, im_high, re_high, im_high, re_low, im_low], axis=0)

    skip = skip_ref[...]
    for k in range(0, outs, 2):
        pair = jnp.concatenate([stacked(group ^ k), stacked(group ^ (k + 1))], axis=1)
        conv = jnp.dot(inv_ref[...], pair, preferred_element_type=F32)
        for i in range(2):
            values = xs_ref[half * outs + (group ^ (k + i))].astype(F32)
            gate = gate_refs[k + i][...].astype(F32)
            mixed = conv[:, i * LANES : (i + 1) * LANES] + skip * values
            out_refs[k + i][...] = (gate * mixed).astype(BF16)


def call_conv(xs, gates, filters, passing):
    blocks, block, _ = xs.shape
    outs = len(gates)
    pinned = [pltpu.with_memory_space_constraint(each, VMEM) for each in filters]
    operands = [xs, *gates, *pinned]
    shape = jax.ShapeDtypeStruct
    return pl.pallas_call(
        functools.partial(conv_kernel, blocks, outs, block),
        in_specs=[pl.BlockSpec(memory_space=VMEM)] * len(operands)
        + [pl.BlockSpec(memory_space=pl.ANY)] * 2,
        out_specs=[pl.BlockSpec(memory_space=VMEM)] * outs
        + [pl.BlockSpec(memory_space=pl.ANY)] * 2,
        out_shape=[shape((block, LANES), BF16)] * outs + [shape(p.shape, p.dtype) for p in passing],
        input_output_aliases={len(operands) + i: outs + i for i in range(2)},
        scratch_shapes=[
            VMEM((blocks, block, LANES), F32),
            VMEM((blocks, block, LANES), F32),
            VMEM((outs, block, LANES), F32),
            VMEM((outs, block, LANES), F32),
        ],
        compiler_params=pltpu.CompilerParams(vmem_limit_bytes=16 * 2**20),
        cost_estimate=pl.CostEstimate(
            flops=2 * 10**8, bytes_accessed=3 * 2**20, transcendentals=0
        ),
        name="convolve",
    )(*operands, *passing)


def join_kernel(outs, *refs):
    piece_refs, joined_ref = refs[:outs], refs[outs]
    group = lax.axis_index("seq") % outs
    for k in range(outs):
        lanes = pl.ds(pl.multiple_of((group ^ k) * LANES, LANES), LANES)
        joined_ref[:, lanes] = piece_refs[k][...]


def tiles(width):
    step = min(width, 2 * LANES)
    return [slice(start, start + step) for start in range(0, width, step)]


def own_kernel(width, gated_ref, weight_ref, *refs):
    out_refs, (held_ref, sems) = refs[:4], refs[4:]
    me = lax.axis_index("chan")
    copies = [
        pltpu.make_async_copy(
            weight_ref.at[:, columns_of(me ^ k, half, width)], held_ref.at[i], sems.at[i]
        )
        for i, (k, half) in enumerate(((2, 0), (1, 1), (0, 0), (0, 1)))
    ]
    for copy in copies:
        copy.start()
    left = gated_ref[...]
    for i, copy in enumerate(copies):
        copy.wait()
        for lanes in tiles(width // 2):
            out_refs[i][:, lanes] = jnp.dot(
                left, held_ref[i, :, lanes], preferred_element_type=F32
            )


def neighbour_kernel(first, x_ref, y_ref, *refs):
    from_x, from_y, sums, outs = refs[:2], refs[2:4], refs[4:6], refs[6:]
    rows = from_x[0].shape[0]
    core = lax.axis_index("seq") % 2
    for left_ref, held, sum_ref, out_ref in (
        (x_ref, from_x, sums[0], outs[0]),
        (y_ref, from_y, sums[1], outs[1]),
    ):
        near = left_ref[:, pl.ds(pl.multiple_of(core * rows, LANES), rows)]
        far = left_ref[:, pl.ds(pl.multiple_of((1 - core) * rows, LANES), rows)]
        width = out_ref.shape[1]
        for lanes in tiles(width):
            place = slice(first * width + lanes.start, first * width + lanes.stop)
            total = jnp.dot(near, held[0][:, place], preferred_element_type=F32)
            total += jnp.dot(far, held[1][:, place], preferred_element_type=F32)
            out_ref[:, lanes] = (sum_ref[:, lanes] + total).astype(out_ref.dtype)


def last_kernel(*refs):
    sums, arrived, out_ref = refs[:2], refs[2:4], refs[4]
    width = sums[0].shape[1]
    for half in range(2):
        out_ref[:, half * width : (half + 1) * width] = (
            sums[half][...] + arrived[half][...].astype(F32)
        ).astype(BF16)


def in_vmem(kernel, operands, out_shape, name, flops, scratch=()):
    return pl.pallas_call(
        kernel,
        in_specs=[pl.BlockSpec(memory_space=VMEM)] * len(operands),
        out_specs=jax.tree.map(lambda _: pl.BlockSpec(memory_space=VMEM), out_shape),
        out_shape=out_shape,
        scratch_shapes=scratch,
        compiler_params=pltpu.CompilerParams(vmem_limit_bytes=16 * 2**20),
        cost_estimate=pl.CostEstimate(flops=flops, bytes_accessed=2**20, transcendentals=0),
        name=name,
    )(*operands)


def call_own(gated, weight):
    block, width = gated.shape
    columns = weight.shape[1] // FACE
    return pl.pallas_call(
        functools.partial(own_kernel, columns),
        in_specs=[pl.BlockSpec(memory_space=VMEM), pl.BlockSpec(memory_space=pltpu.HBM)],
        out_specs=[pl.BlockSpec(memory_space=VMEM)] * 4,
        out_shape=[jax.ShapeDtypeStruct((block, columns // 2), F32)] * 4,
        scratch_shapes=[
            VMEM((4, width, columns // 2), BF16),
            pltpu.SemaphoreType.DMA((4,)),
        ],
        compiler_params=pltpu.CompilerParams(vmem_limit_bytes=16 * 2**20),
        cost_estimate=pl.CostEstimate(
            flops=4 * block * width * columns, bytes_accessed=6 * width * columns, transcendentals=0
        ),
        name="own_channels",
    )(gated, pltpu.with_memory_space_constraint(weight, pltpu.HBM))


def split_shards(
    mixer_input,
    gate_branch,
    skip_gain,
    decay_rate,
    first_weight,
    first_bias,
    second_weight,
    second_bias,
    last_weight,
    output_weight,
):
    block, width = mixer_input.shape
    blocks = lax.axis_size("seq")
    outs = width // LANES

    along_seq = lambda part, k: lax.ppermute(part, "seq", [(s, s ^ k) for s in range(blocks)])
    along_chan = lambda part, k: lax.ppermute(part, "chan", [(c, c ^ k) for c in range(FACE)])
    to_partners = lambda parts: [parts[0]] + [along_seq(parts[k], k) for k in range(1, outs)]

    xs, *gates, over_x, over_y = call_pack(
        mixer_input, gate_branch, output_weight, blocks, outs
    )
    xs = lax.all_to_all(xs, "seq", 0, 0, tiled=True)
    from_x, from_y = along_chan(over_x, 1), along_chan(over_y, 2)
    filters = call_filter(
        (first_weight, first_bias, second_weight, second_bias, last_weight, decay_rate),
        skip_gain,
        blocks,
        outs,
        block,
    )
    *pieces, from_x, from_y = call_conv(xs, to_partners(gates), filters, (from_x, from_y))
    from_x, from_y = (from_x, along_seq(from_x, 1)), (from_y, along_seq(from_y, 1))
    pieces = to_partners(pieces)
    shape = jax.ShapeDtypeStruct
    gated = in_vmem(
        functools.partial(join_kernel, outs),
        pieces,
        shape((block, width), BF16),
        "join_pieces",
        10**6,
    )
    x_gated, y_gated = along_chan(gated, 1), along_chan(gated, 2)
    send_a, send_b, keep_a, keep_b = call_own(gated, output_weight)
    columns = send_a.shape[1]
    flops = 4 * block * width * columns
    send_a, send_b = in_vmem(
        functools.partial(neighbour_kernel, 1),
        [x_gated, y_gated, *from_x, *from_y, send_a, send_b],
        [shape((block, columns), BF16)] * 2,
        "sums_to_send",
        flops,
    )
    got_a, got_b = along_chan(send_a, 2), along_chan(send_b, 1)
    keep_a, keep_b = in_vmem(
        functools.partial(neighbour_kernel, 0),
        [x_gated, y_gated, *from_x, *from_y, keep_a, keep_b],
        [shape((block, columns), F32)] * 2,
        "sums_to_keep",
        flops,
    )
    return in_vmem(
        last_kernel,
        [keep_a, keep_b, got_a, got_b],
        shape((block, 2 * columns), BF16),
        "last_sum",
        10**6,
    )


def contract_first(left_matrix, right_matrix):
    return lax.dot_general(
        left_matrix,
        right_matrix,
        (((0,), (0,)), ((), ())),
        precision=HIGHEST,
        preferred_element_type=F32,
    )


def filter_taps(
    first_weight, first_bias, second_weight, second_bias, last_weight, decay_rate, length
):
    features = jnp.asarray(feature_table(length, first_weight.shape[0]).T)
    hidden_one = jnp.sin(contract_first(first_weight, features) + first_bias[:, None])
    hidden_two = jnp.sin(contract_first(second_weight, hidden_one) + second_bias[:, None])
    shaped = contract_first(hidden_two, last_weight)
    positions = jnp.arange(length, dtype=jnp.int32).astype(F32)
    envelope = jnp.exp(-decay_rate[None, :] * (positions[:, None] / length))
    energy = jnp.expm1(-2.0 * decay_rate) / jnp.expm1(-2.0 * decay_rate / length)
    return shaped * envelope / jnp.sqrt(energy)[None, :]


def transform_tables(block_len):
    padded_len = 2 * block_len
    freq_index = jnp.arange(block_len + 1, dtype=jnp.int32)[:, None]
    time_index = jnp.arange(padded_len, dtype=jnp.int32)[None, :]
    angle = (freq_index * time_index % padded_len).astype(F32) * (2.0 * math.pi / padded_len)
    forward = jnp.concatenate([jnp.cos(angle), -jnp.sin(angle)], axis=0)
    later_angle = angle[:, block_len:]
    weights = jnp.where((freq_index == 0) | (freq_index == block_len), 1.0, 2.0) / padded_len
    inverse = jnp.concatenate(
        [(weights * jnp.cos(later_angle)).T, (-weights * jnp.sin(later_angle)).T], axis=1
    )
    return (forward, inverse)


def spectral_product(left_spec, right_spec, half_rows):
    left_real, left_imag = (left_spec[:half_rows], left_spec[half_rows:])
    right_real, right_imag = (right_spec[:half_rows], right_spec[half_rows:])
    return jnp.concatenate(
        [
            left_real * right_real - left_imag * right_imag,
            left_real * right_imag + left_imag * right_real,
        ],
        axis=0,
    )


def gathered_shards(
    mixer_input,
    gate_branch,
    skip_gain,
    decay_rate,
    first_weight,
    first_bias,
    second_weight,
    second_bias,
    last_weight,
    output_weight,
):
    block_len, chan_width = mixer_input.shape
    seq_count = lax.axis_size("seq")
    device = lax.axis_index("seq")
    half_rows = block_len + 1
    kernel_taps = filter_taps(
        first_weight,
        first_bias,
        second_weight,
        second_bias,
        last_weight,
        decay_rate,
        block_len * seq_count,
    )
    padded_taps = jnp.concatenate([jnp.zeros((block_len, chan_width), F32), kernel_taps], axis=0)
    forward, inverse = transform_tables(block_len)
    forward_head = forward[:, :block_len]
    gathered = lax.all_gather(mixer_input, "seq", axis=0, tiled=True)

    def one_block(block_index, total):
        rows = lax.dynamic_slice_in_dim(gathered, block_index * block_len, block_len, 0)
        source_spec = jnp.dot(
            forward_head, rows.astype(F32), precision=HIGHEST, preferred_element_type=F32
        )
        segment = lax.dynamic_slice_in_dim(
            padded_taps, (device - block_index) * block_len, 2 * block_len, 0
        )
        lag_spec = jnp.dot(forward, segment, precision=HIGHEST, preferred_element_type=F32)
        return total + spectral_product(lag_spec, source_spec, half_rows)

    total = lax.fori_loop(0, device + 1, one_block, jnp.zeros((2 * half_rows, chan_width), F32))
    convolved = jnp.dot(inverse, total, precision=HIGHEST, preferred_element_type=F32)
    values = mixer_input.astype(F32)
    gated_mix = (
        gate_branch.astype(F32) * (convolved + skip_gain[None, :] * values)
    ).astype(BF16)
    partial_out = jnp.dot(gated_mix, output_weight, preferred_element_type=F32)
    return lax.psum_scatter(partial_out, "chan", scatter_dimension=1, tiled=True).astype(BF16)


def solution(mesh):
    seq_count, chan_count = mesh.shape["seq"], mesh.shape["chan"]

    def shards(mixer_input, *rest):
        block, width = mixer_input.shape
        outs = width // LANES
        splits = (
            width % LANES == 0
            and block % LANES == 0
            and seq_count == 2 * outs
            and outs == 4
            and chan_count == FACE
        )
        plan = split_shards if splits else gathered_shards
        return plan(mixer_input, *rest)

    in_specs = (
        P("seq", "chan"),
        P("seq", "chan"),
        P("chan"),
        P("chan"),
        P(),
        P(),
        P(),
        P(),
        P(None, "chan"),
        P("chan", None),
    )
    out_specs = P("seq", "chan")
    return jax.shard_map(shards, mesh=mesh, in_specs=in_specs, out_specs=out_specs, check_vma=False)
```

profile of v0, /device:TPU:0, one launch (start us, length us, event | category | flops | bytes accessed | tf_op | source)
XLA Modules:
  0.0 42.0 jit_solution(16623112280001414580)
XLA Ops:
  0.0 2.5 %pack_pieces.1 = (bf16[8,128,128]{2,1,0:T(8,128)(2,1)}, bf16[128,128]{1,0:T(8,128)(2,1)}, bf16[128,128]{1,0:T(8,128)(2,1)}, bf16[128,128]{1,0:T(8,128)(2,1)}, bf...) custom-call(bf16[128,512]{1,0:T(8,128)(2,1)} %x_ref.1, ...), custom_call_target="tpu_custom_call" | custom-call | bytes 2097152 | tf_op jit(solution)/shard_map/pack_pieces/pallas_call | solution.py:284
  2.5 3.0 %collective-permute-start.3 = (bf16[256,1024]{1,0:T(8,128)(2,1)}, bf16[256,1024]{1,0:T(8,128)(2,1)S(1)}, u32[]{:S(2)}, u32[]{:S(2)}) collective-permute-start(bf16[256,1024]{1,0:T(8,128)(2,1)} %get-tuple-element.43), channel_id=1, source_target_pairs={{0,1},{1,0},{2,3},{3,2},{4,5},{5,4},{6,7},{7,6},{8,9},{9,8},{10,11... | collective-permute-start | bytes 1572872 | tf_op jit(solution)/shard_map/ppermute | solution.py:492
  5.5 1.5 %collective-permute-start.4 = (bf16[256,1024]{1,0:T(8,128)(2,1)S(1)}, bf16[256,1024]{1,0:T(8,128)(2,1)S(1)}, u32[]{:S(2)}, u32[]{:S(2)}) collective-permute-start(bf16[256,1024]{1,0:T(8,128)(2,1)S(1)} %get-tuple-element.44), channel_id=1, source_target_pairs={{0,2},{1,3},{2,0},{3,1},{4,6},{5,7},{6,4},{7,5},{8,10},{9,11},{10,... | collective-permute-start | bytes 1572872 | tf_op jit(solution)/shard_map/ppermute | solution.py:492
  7.0 4.9 %all-to-all-start = ((bf16[8,128,128]{2,1,0:T(8,128)(2,1)}), bf16[8,128,128]{2,1,0:T(8,128)(2,1)S(1)}, u32[]{:S(2)}, u32[]{:S(2)}) async-start(bf16[8,128,128]{2,1,0:T(8,128)(2,1)} %get-tuple-element.32), calls=%async_computation | async-start | bytes 524288 | tf_op jit(solution)/shard_map/all_to_all | solution.py:498
  11.9 0.5 %collective-permute-start = (bf16[128,128]{1,0:T(8,128)(2,1)}, bf16[128,128]{1,0:T(8,128)(2,1)S(1)}, u32[]{:S(2)}, u32[]{:S(2)}) collective-permute-start(bf16[128,128]{1,0:T(8,128)(2,1)} %get-tuple-element.34), channel_id=1, source_target_pairs={{0,4},{4,0},{8,12},{12,8},{16,20},{20,16},{24,28},{28,24},{1,5},{5... | collective-permute-start | bytes 98312 | tf_op jit(solution)/shard_map/ppermute | solution.py:491
  12.4 1.7 %collective-permute-start.1 = (bf16[128,128]{1,0:T(8,128)(2,1)}, bf16[128,128]{1,0:T(8,128)(2,1)S(1)}, u32[]{:S(2)}, u32[]{:S(2)}) collective-permute-start(bf16[128,128]{1,0:T(8,128)(2,1)} %get-tuple-element.35), channel_id=1, source_target_pairs={{0,8},{4,12},{8,0},{12,4},{16,24},{20,28},{24,16},{28,20},{1,9},{5... | collective-permute-start | bytes 98312 | tf_op jit(solution)/shard_map/ppermute | solution.py:491
  14.1 0.0 collective-permute-start.2
  14.1 2.8 %filter_spectra.1 = (f32[8,128,128]{2,1,0:T(8,128)S(1)}, f32[8,128,128]{2,1,0:T(8,128)S(1)}, f32[8,8,128]{2,1,0:T(8,128)S(1)}, bf16[256,256]{1,0:T(8,128)(2,1)S(...) custom-call(f32[33,64]{1,0:T(8,128)} %refs_0_.1, f32[512,240]{1,0:T(8,128)} %constant.6.clone.refs_1_, ...), custom_call_target="tpu_custom_call" | custom-call | flops 400000000 | bytes 8388608 | tf_op jit(solution)/shard_map/filter_spectra/pallas_call | solution.py:209
  17.0 0.0 collective-permute-done.refs_1_
  17.0 1.3 %collective-permute-done.1.refs_2_ = bf16[128,128]{1,0:T(8,128)(2,1)S(1)} collective-permute-done((bf16[128,128]{1,0:T(8,128)(2,1)}, bf16[128,128]{1,0:T(8,128)(2,1)S(1)}, u32[]{:S(2)}, u32[]{:S(2)}) %collective-permute-start.1) | collective-permute-done | bytes 32800 | tf_op jit(solution)/shard_map/ppermute | solution.py:491
  18.2 0.5 %collective-permute-done.2.refs_3_ = bf16[128,128]{1,0:T(8,128)(2,1)S(1)} collective-permute-done((bf16[128,128]{1,0:T(8,128)(2,1)}, bf16[128,128]{1,0:T(8,128)(2,1)S(1)}, u32[]{:S(2)}, u32[]{:S(2)}) %collective-permute-start.2) | collective-permute-done | bytes 32800 | tf_op jit(solution)/shard_map/ppermute | solution.py:491
  18.7 2.9 %all-to-all-done.xs_ref = bf16[8,128,128]{2,1,0:T(8,128)(2,1)S(1)} async-done(((bf16[8,128,128]{2,1,0:T(8,128)(2,1)}), bf16[8,128,128]{2,1,0:T(8,128)(2,1)S(1)}, u32[]{:S(2)}, u32[]{:S(2)}) %all-to-all-start) | async-done | bytes 262176 | tf_op jit(solution)/shard_map/all_to_all | solution.py:498
  21.6 0.0 collective-permute-done.3.refs_10_
  21.6 0.0 collective-permute-done.4.refs_11_
  21.6 0.0 copy-start
  21.6 0.8 %copy-done = bf16[128,128]{1,0:T(8,128)(2,1)S(1)} copy-done((bf16[128,128]{1,0:T(8,128)(2,1)S(1)}, bf16[128,128]{1,0:T(8,128)(2,1)}, u32[]{:S(2)}) %copy-start) | copy-done | bytes 32792
  22.4 1.2 %convolve.1 = (bf16[128,128]{1,0:T(8,128)(2,1)S(1)}, bf16[128,128]{1,0:T(8,128)(2,1)S(1)}, bf16[128,128]{1,0:T(8,128)(2,1)S(1)}, bf16[128,128]{1,0:T(8,128)(2,1)...) custom-call(bf16[8,128,128]{2,1,0:T(8,128)(2,1)S(1)} %all-to-all-don, ...), custom_call_target="tpu_custom_call", output_to_operand_aliasing={{4}: (11, {}), {5}: (12, {})} | custom-call | flops 200000000 | bytes 3145728 | tf_op jit(solution)/shard_map/convolve/pallas_call | solution.py:360
  23.6 0.1 collective-permute-start.10
  23.7 0.5 %collective-permute-start.11 = (bf16[256,1024]{1,0:T(8,128)(2,1)S(1)}, bf16[256,1024]{1,0:T(8,128)(2,1)S(1)}, u32[]{:S(2)}, u32[]{:S(2)}) collective-permute-start(bf16[256,1024]{1,0:T(8,128)(2,1)S(1)} %get-tuple-element.50.refs_2_), channel_id=1, source_target_pairs={{0,4},{4,0},{8,12},{12,8},{16,20},{20,16},{24,28},{28,24},{1,5},{5... | collective-permute-start | bytes 1572872 | tf_op jit(solution)/shard_map/ppermute | solution.py:491
  24.2 0.1 collective-permute-start.5
  24.2 0.6 %collective-permute-start.6 = (bf16[128,128]{1,0:T(8,128)(2,1)S(1)}, bf16[128,128]{1,0:T(8,128)(2,1)S(1)}, u32[]{:S(2)}, u32[]{:S(2)}) collective-permute-start(bf16[128,128]{1,0:T(8,128)(2,1)S(1)} %get-tuple-element.47), channel_id=1, source_target_pairs={{0,8},{4,12},{8,0},{12,4},{16,24},{20,28},{24,16},{28,20},{1,9},{5... | collective-permute-start | bytes 98312 | tf_op jit(solution)/shard_map/ppermute | solution.py:491
  24.8 1.2 %collective-permute-start.7 = (bf16[128,128]{1,0:T(8,128)(2,1)S(1)}, bf16[128,128]{1,0:T(8,128)(2,1)S(1)}, u32[]{:S(2)}, u32[]{:S(2)}) collective-permute-start(bf16[128,128]{1,0:T(8,128)(2,1)S(1)} %get-tuple-element.48), channel_id=1, source_target_pairs={{0,12},{4,8},{8,4},{12,0},{16,28},{20,24},{24,20},{28,16},{1,13},{... | collective-permute-start | bytes 98312 | tf_op jit(solution)/shard_map/ppermute | solution.py:491
  26.0 0.3 collective-permute-done.5.refs_1_
  26.3 2.1 %collective-permute-done.6.refs_2_ = bf16[128,128]{1,0:T(8,128)(2,1)S(1)} collective-permute-done((bf16[128,128]{1,0:T(8,128)(2,1)S(1)}, bf16[128,128]{1,0:T(8,128)(2,1)S(1)}, u32[]{:S(2)}, u32[]{:S(2)}) %collective-permute-start.6) | collective-permute-done | bytes 32800 | tf_op jit(solution)/shard_map/ppermute | solution.py:491
  28.5 0.0 collective-permute-done.7.refs_3_
  28.6 0.6 %collective-permute-start.9 = (bf16[128,512]{1,0:T(8,128)(2,1)S(1)}, bf16[128,512]{1,0:T(8,128)(2,1)S(1)}, u32[]{:S(2)}, u32[]{:S(2)}) collective-permute-start(bf16[128,512]{1,0:T(8,128)(2,1)S(1)} %join_pieces.1.gated_ref), channel_id=1, source_target_pairs={{0,2},{1,3},{2,0},{3,1},{4,6},{5,7},{6,4},{7,5},{8,10},{9,11},{10,... | collective-permute-start | bytes 393224 | tf_op jit(solution)/shard_map/ppermute | solution.py:492
  29.1 0.5 %collective-permute-start.8 = (bf16[128,512]{1,0:T(8,128)(2,1)S(1)}, bf16[128,512]{1,0:T(8,128)(2,1)S(1)}, u32[]{:S(2)}, u32[]{:S(2)}) collective-permute-start(bf16[128,512]{1,0:T(8,128)(2,1)S(1)} %join_pieces.1.gated_ref), channel_id=1, source_target_pairs={{0,1},{1,0},{2,3},{3,2},{4,5},{5,4},{6,7},{7,6},{8,9},{9,8},{10,11... | collective-permute-start | bytes 393224 | tf_op jit(solution)/shard_map/ppermute | solution.py:492
  29.7 2.0 %own_channels.1 = (f32[128,512]{1,0:T(8,128)S(1)}, f32[128,512]{1,0:T(8,128)S(1)}, f32[128,512]{1,0:T(8,128)S(1)}, f32[128,512]{1,0:T(8,128)S(1)}) custom-call(bf16[128,512]{1,0:T(8,128)(2,1)S(1)} %join_pieces.1.gated_ref, bf16[512,4096]{1,0:T(8,128)(2,1)} %weight_ref.3), custom_call_target="tpu_custom_call" | custom-call | flops 268435456 | bytes 3145728 | tf_op jit(solution)/shard_map/own_channels/pallas_call | solution.py:458
  31.7 2.5 %collective-permute-done.9.y_ref = bf16[128,512]{1,0:T(8,128)(2,1)S(1)} collective-permute-done((bf16[128,512]{1,0:T(8,128)(2,1)S(1)}, bf16[128,512]{1,0:T(8,128)(2,1)S(1)}, u32[]{:S(2)}, u32[]{:S(2)}) %collective-permute-start.9) | collective-permute-done | bytes 131104 | tf_op jit(solution)/shard_map/ppermute | solution.py:492
  34.2 0.2 collective-permute-done.8.x_ref
  34.4 0.0 collective-permute-done.10.refs_1_
  34.4 0.0 collective-permute-done.11.refs_3_
  34.4 0.3 sums_to_send.1
  34.7 1.6 %collective-permute-start.12 = (bf16[128,512]{1,0:T(8,128)(2,1)S(1)}, bf16[128,512]{1,0:T(8,128)(2,1)S(1)}, u32[]{:S(2)}, u32[]{:S(2)}) collective-permute-start(bf16[128,512]{1,0:T(8,128)(2,1)S(1)} %get-tuple-element.57), channel_id=1, source_target_pairs={{0,2},{1,3},{2,0},{3,1},{4,6},{5,7},{6,4},{7,5},{8,10},{9,11},{10,... | collective-permute-start | bytes 393224 | tf_op jit(solution)/shard_map/ppermute | solution.py:492
  36.3 0.5 %collective-permute-start.13 = (bf16[128,512]{1,0:T(8,128)(2,1)S(1)}, bf16[128,512]{1,0:T(8,128)(2,1)S(1)}, u32[]{:S(2)}, u32[]{:S(2)}) collective-permute-start(bf16[128,512]{1,0:T(8,128)(2,1)S(1)} %get-tuple-element.58), channel_id=1, source_target_pairs={{0,1},{1,0},{2,3},{3,2},{4,5},{5,4},{6,7},{7,6},{8,9},{9,8},{10,11... | collective-permute-start | bytes 393224 | tf_op jit(solution)/shard_map/ppermute | solution.py:492
  36.9 0.3 sums_to_keep.1
  37.2 2.6 %collective-permute-done.12.refs_2_ = bf16[128,512]{1,0:T(8,128)(2,1)S(1)} collective-permute-done((bf16[128,512]{1,0:T(8,128)(2,1)S(1)}, bf16[128,512]{1,0:T(8,128)(2,1)S(1)}, u32[]{:S(2)}, u32[]{:S(2)}) %collective-permute-start.12) | collective-permute-done | bytes 131104 | tf_op jit(solution)/shard_map/ppermute | solution.py:492
  39.8 1.5 %collective-permute-done.13.refs_3_ = bf16[128,512]{1,0:T(8,128)(2,1)S(1)} collective-permute-done((bf16[128,512]{1,0:T(8,128)(2,1)S(1)}, bf16[128,512]{1,0:T(8,128)(2,1)S(1)}, u32[]{:S(2)}, u32[]{:S(2)}) %collective-permute-start.13) | collective-permute-done | bytes 131104 | tf_op jit(solution)/shard_map/ppermute | solution.py:492
  41.3 0.7 %last_sum.1 = bf16[128,1024]{1,0:T(8,128)(2,1)} custom-call(f32[128,512]{1,0:T(8,128)S(1)} %get-tuple-element.53.refs_0_, f32[128,512]{1,0:T(8,128)S(1)} %get-tuple-element.54.refs_1_, bf16[128,512]{1,0:T(8,128)(2,1)S(1)} %collective-permute-done.12.refs_2_, bf16[128,512]{1,0:T(8,128)(2,1)S(1)} %collective-permute-done.13.refs_3_), custom_call_target="tpu_custom_call" | custom-call | flops 1000000 | bytes 1048576 | tf_op jit(solution)/shard_map/last_sum/pallas_call | solution.py:443
  (1 shorter events, 0.0 us)
Async XLA Ops:
  2.5 19.1 %collective-permute-start.3 = (bf16[256,1024]{1,0:T(8,128)(2,1)}, bf16[256,1024]{1,0:T(8,128)(2,1)S(1)}, u32[]{:S(2)}, u32[]{:S(2)}) collective-permute-start(bf16[256,1024]{1,0:T(8,128)(2,1)} %get-tuple-element.43), channel_id=1, source_target_pairs={{0,1},{1,0},{2,3},{3,2},{4,5},{5,4},{6,7},{7,6},{8,9},{9,8},{10,11... | collective-permute-start | bytes 1572872 | tf_op jit(solution)/shard_map/ppermute | solution.py:492
  5.5 16.1 %collective-permute-start.4 = (bf16[256,1024]{1,0:T(8,128)(2,1)S(1)}, bf16[256,1024]{1,0:T(8,128)(2,1)S(1)}, u32[]{:S(2)}, u32[]{:S(2)}) collective-permute-start(bf16[256,1024]{1,0:T(8,128)(2,1)S(1)} %get-tuple-element.44), channel_id=1, source_target_pairs={{0,2},{1,3},{2,0},{3,1},{4,6},{5,7},{6,4},{7,5},{8,10},{9,11},{10,... | collective-permute-start | bytes 1572872 | tf_op jit(solution)/shard_map/ppermute | solution.py:492
  7.0 14.6 %all-to-all-start = ((bf16[8,128,128]{2,1,0:T(8,128)(2,1)}), bf16[8,128,128]{2,1,0:T(8,128)(2,1)S(1)}, u32[]{:S(2)}, u32[]{:S(2)}) async-start(bf16[8,128,128]{2,1,0:T(8,128)(2,1)} %get-tuple-element.32), calls=%async_computation | async-start | bytes 524288 | tf_op jit(solution)/shard_map/all_to_all | solution.py:498
  11.9 5.0 %collective-permute-start = (bf16[128,128]{1,0:T(8,128)(2,1)}, bf16[128,128]{1,0:T(8,128)(2,1)S(1)}, u32[]{:S(2)}, u32[]{:S(2)}) collective-permute-start(bf16[128,128]{1,0:T(8,128)(2,1)} %get-tuple-element.34), channel_id=1, source_target_pairs={{0,4},{4,0},{8,12},{12,8},{16,20},{20,16},{24,28},{28,24},{1,5},{5... | collective-permute-start | bytes 98312 | tf_op jit(solution)/shard_map/ppermute | solution.py:491
  12.4 5.8 %collective-permute-start.1 = (bf16[128,128]{1,0:T(8,128)(2,1)}, bf16[128,128]{1,0:T(8,128)(2,1)S(1)}, u32[]{:S(2)}, u32[]{:S(2)}) collective-permute-start(bf16[128,128]{1,0:T(8,128)(2,1)} %get-tuple-element.35), channel_id=1, source_target_pairs={{0,8},{4,12},{8,0},{12,4},{16,24},{20,28},{24,16},{28,20},{1,9},{5... | collective-permute-start | bytes 98312 | tf_op jit(solution)/shard_map/ppermute | solution.py:491
  14.1 4.6 %collective-permute-start.2 = (bf16[128,128]{1,0:T(8,128)(2,1)}, bf16[128,128]{1,0:T(8,128)(2,1)S(1)}, u32[]{:S(2)}, u32[]{:S(2)}) collective-permute-start(bf16[128,128]{1,0:T(8,128)(2,1)} %get-tuple-element.36), channel_id=1, source_target_pairs={{0,12},{4,8},{8,4},{12,0},{16,28},{20,24},{24,20},{28,16},{1,13},{... | collective-permute-start | bytes 98312 | tf_op jit(solution)/shard_map/ppermute | solution.py:491
  21.6 0.8 %copy-start = (bf16[128,128]{1,0:T(8,128)(2,1)S(1)}, bf16[128,128]{1,0:T(8,128)(2,1)}, u32[]{:S(2)}) copy-start(bf16[128,128]{1,0:T(8,128)(2,1)} %get-tuple-element.33.refs_0_) | copy-start | bytes 98308
  23.6 10.8 %collective-permute-start.10 = (bf16[256,1024]{1,0:T(8,128)(2,1)S(1)}, bf16[256,1024]{1,0:T(8,128)(2,1)S(1)}, u32[]{:S(2)}, u32[]{:S(2)}) collective-permute-start(bf16[256,1024]{1,0:T(8,128)(2,1)S(1)} %get-tuple-element.49.refs_0_), channel_id=1, source_target_pairs={{0,4},{4,0},{8,12},{12,8},{16,20},{20,16},{24,28},{28,24},{1,5},{5... | collective-permute-start | bytes 1572872 | tf_op jit(solution)/shard_map/ppermute | solution.py:491
  23.7 10.8 %collective-permute-start.11 = (bf16[256,1024]{1,0:T(8,128)(2,1)S(1)}, bf16[256,1024]{1,0:T(8,128)(2,1)S(1)}, u32[]{:S(2)}, u32[]{:S(2)}) collective-permute-start(bf16[256,1024]{1,0:T(8,128)(2,1)S(1)} %get-tuple-element.50.refs_2_), channel_id=1, source_target_pairs={{0,4},{4,0},{8,12},{12,8},{16,20},{20,16},{24,28},{28,24},{1,5},{5... | collective-permute-start | bytes 1572872 | tf_op jit(solution)/shard_map/ppermute | solution.py:491
  24.2 2.2 %collective-permute-start.5 = (bf16[128,128]{1,0:T(8,128)(2,1)S(1)}, bf16[128,128]{1,0:T(8,128)(2,1)S(1)}, u32[]{:S(2)}, u32[]{:S(2)}) collective-permute-start(bf16[128,128]{1,0:T(8,128)(2,1)S(1)} %get-tuple-element.46), channel_id=1, source_target_pairs={{0,4},{4,0},{8,12},{12,8},{16,20},{20,16},{24,28},{28,24},{1,5},{5... | collective-permute-start | bytes 98312 | tf_op jit(solution)/shard_map/ppermute | solution.py:491
  24.2 4.2 %collective-permute-start.6 = (bf16[128,128]{1,0:T(8,128)(2,1)S(1)}, bf16[128,128]{1,0:T(8,128)(2,1)S(1)}, u32[]{:S(2)}, u32[]{:S(2)}) collective-permute-start(bf16[128,128]{1,0:T(8,128)(2,1)S(1)} %get-tuple-element.47), channel_id=1, source_target_pairs={{0,8},{4,12},{8,0},{12,4},{16,24},{20,28},{24,16},{28,20},{1,9},{5... | collective-permute-start | bytes 98312 | tf_op jit(solution)/shard_map/ppermute | solution.py:491
  24.8 3.7 %collective-permute-start.7 = (bf16[128,128]{1,0:T(8,128)(2,1)S(1)}, bf16[128,128]{1,0:T(8,128)(2,1)S(1)}, u32[]{:S(2)}, u32[]{:S(2)}) collective-permute-start(bf16[128,128]{1,0:T(8,128)(2,1)S(1)} %get-tuple-element.48), channel_id=1, source_target_pairs={{0,12},{4,8},{8,4},{12,0},{16,28},{20,24},{24,20},{28,16},{1,13},{... | collective-permute-start | bytes 98312 | tf_op jit(solution)/shard_map/ppermute | solution.py:491
  28.6 5.6 %collective-permute-start.9 = (bf16[128,512]{1,0:T(8,128)(2,1)S(1)}, bf16[128,512]{1,0:T(8,128)(2,1)S(1)}, u32[]{:S(2)}, u32[]{:S(2)}) collective-permute-start(bf16[128,512]{1,0:T(8,128)(2,1)S(1)} %join_pieces.1.gated_ref), channel_id=1, source_target_pairs={{0,2},{1,3},{2,0},{3,1},{4,6},{5,7},{6,4},{7,5},{8,10},{9,11},{10,... | collective-permute-start | bytes 393224 | tf_op jit(solution)/shard_map/ppermute | solution.py:492
  29.1 5.3 %collective-permute-start.8 = (bf16[128,512]{1,0:T(8,128)(2,1)S(1)}, bf16[128,512]{1,0:T(8,128)(2,1)S(1)}, u32[]{:S(2)}, u32[]{:S(2)}) collective-permute-start(bf16[128,512]{1,0:T(8,128)(2,1)S(1)} %join_pieces.1.gated_ref), channel_id=1, source_target_pairs={{0,1},{1,0},{2,3},{3,2},{4,5},{5,4},{6,7},{7,6},{8,9},{9,8},{10,11... | collective-permute-start | bytes 393224 | tf_op jit(solution)/shard_map/ppermute | solution.py:492
  34.7 5.0 %collective-permute-start.12 = (bf16[128,512]{1,0:T(8,128)(2,1)S(1)}, bf16[128,512]{1,0:T(8,128)(2,1)S(1)}, u32[]{:S(2)}, u32[]{:S(2)}) collective-permute-start(bf16[128,512]{1,0:T(8,128)(2,1)S(1)} %get-tuple-element.57), channel_id=1, source_target_pairs={{0,2},{1,3},{2,0},{3,1},{4,6},{5,7},{6,4},{7,5},{8,10},{9,11},{10,... | collective-permute-start | bytes 393224 | tf_op jit(solution)/shard_map/ppermute | solution.py:492
  36.3 5.0 %collective-permute-start.13 = (bf16[128,512]{1,0:T(8,128)(2,1)S(1)}, bf16[128,512]{1,0:T(8,128)(2,1)S(1)}, u32[]{:S(2)}, u32[]{:S(2)}) collective-permute-start(bf16[128,512]{1,0:T(8,128)(2,1)S(1)} %get-tuple-element.58), channel_id=1, source_target_pairs={{0,1},{1,0},{2,3},{3,2},{4,5},{5,4},{6,7},{7,6},{8,9},{9,8},{10,11... | collective-permute-start | bytes 393224 | tf_op jit(solution)/shard_map/ppermute | solution.py:492
where the time goes:
time: 42.4 us; the launch traced here: 42 us
  starting transfers between devices  17.3 us (41%)
  waiting for transfers between devices  14 us (33%)
  Pallas kernels  9.94 us (23%)
  local copies, waits for them, and re-layouts  0.76 us (2%)
    ppermute x6, starting transfers between devices, split_shards(): lax.ppermute(part, 'chan', [(c, c ^ k) for c in range(FACE)])  7.76 us
    ppermute x6, waiting for transfers between devices, split_shards(): lax.ppermute(part, 'chan', [(c, c ^ k) for c in range(FACE)])  6.82 us
    all_to_all x1, starting transfers between devices, split_shards(): xs = lax.all_to_all(xs, 'seq', 0, 0, tiled=True)  4.88 us
    ppermute x8, starting transfers between devices, split_shards(): lax.ppermute(part, 'seq', [(s, s ^ k) for s in range(blocks)])  4.63 us
    ppermute x8, waiting for transfers between devices, split_shards(): lax.ppermute(part, 'seq', [(s, s ^ k) for s in range(blocks)])  4.27 us
    all_to_all x1, waiting for transfers between devices, split_shards(): xs = lax.all_to_all(xs, 'seq', 0, 0, tiled=True)  2.89 us
    pallas_call x1, Pallas kernels, call_filter(): pl.pallas_call(functools.partial(filter_kernel, blocks, block, outs, pad)...  2.84 us
    pallas_call x1, Pallas kernels, call_pack(): pl.pallas_call(functools.partial(pack_kernel, blocks, outs), in_specs=[pl...  2.5 us
  transfers between devices with their start and end apart: 15, of which 9 were waited for; matrix products, arithmetic and copies ran while one was open for 0% of the time, Pallas kernels for 12%

commit v1 on v0

--- a/solution.py
+++ b/solution.py
@@ -13,6 +13,9 @@
 F32 = jnp.float32
 BF16 = jnp.bfloat16
 LANES = 128
+WIDE = 2 * LANES
+CORES = 2
+CHIPS = 4
 FACE = 4
 VMEM = pltpu.VMEM
 
@@ -110,8 +113,8 @@
     )
 
 
-def filter_kernel(blocks, block, outs, pad, *refs):
-    hbm, refs = refs[:10], refs[10:]
+def filter_kernel(blocks, block, pad, *refs):
+    hbm, refs = refs[:10], refs[11:]
     hre_ref, him_ref, hfirst_ref, fwd_ref, inv_ref, skip_ref = refs[:6]
     refs = refs[6:]
     w1_ref, b1_ref, w2_ref, b2_ref, w3_ref, decay_ref, feat_ref, table_ref, back_ref = refs[:9]
@@ -125,7 +128,7 @@
     ]
     for copy in copies:
         copy.start()
-    group = lax.axis_index("seq") % outs
+    core = lax.axis_index("seq") % CORES
     length = blocks * block
     emb, order = w1_ref.shape
     first_ref[...] = jnp.zeros_like(first_ref)
@@ -147,12 +150,12 @@
         + b1
     )
     hidden = fast_sin(layer(hidden, stacked_diagonal(w2_ref[...])) + b2)
-    lanes = pl.ds(pl.multiple_of(group * LANES, LANES), LANES)
+    lanes = pl.ds(pl.multiple_of(core * WIDE, LANES), WIDE)
     shaped = layer(hidden, stacked_diagonal(w3_ref[:, lanes]))
 
     decay = decay_ref[:, lanes]
     energy = expm1_of_negative(-2.0 * decay) / expm1_of_negative(decay * (-2.0 / length))
-    times = lax.broadcasted_iota(jnp.int32, (length // 2, LANES), 0).astype(F32) * (1.0 / length)
+    times = lax.broadcasted_iota(jnp.int32, (length // 2, WIDE), 0).astype(F32) * (1.0 / length)
     window = jnp.exp(-(decay * times)) * (1.0 / jnp.sqrt(energy))
     window = jnp.concatenate([window, window * jnp.exp(-0.5 * decay)], axis=1)
     taps_high, taps_low = split_value(shaped * window)
@@ -162,15 +165,15 @@
     fwd_ref[:, :block] = high
     fwd_ref[:, block:] = low
     table = jnp.concatenate([high, low, high], axis=1)
-    rows = lax.broadcasted_iota(jnp.int32, (2 * block, LANES), 0)
+    rows = lax.broadcasted_iota(jnp.int32, (2 * block, WIDE), 0)
     sign = (1 - 2 * lax.rem(rows, 2)).astype(F32)
-    first_row = lax.broadcasted_iota(jnp.int32, (block, LANES), 0) == 0
+    first_row = lax.broadcasted_iota(jnp.int32, (block, WIDE), 0) == 0
     spectra = [None] * blocks
     for k in range(blocks // 2):
         part = slice(k * block, (k + 1) * block)
         stacked = jnp.concatenate([taps_high[part], taps_high[part], taps_low[part]], axis=0)
         now = jnp.dot(table, stacked, preferred_element_type=F32)
-        spectra[k], spectra[k + blocks // 2] = now[:, :LANES], now[:, LANES:]
+        spectra[k], spectra[k + blocks // 2] = now[:, :WIDE], now[:, WIDE:]
     for k in range(blocks):
         spec = spectra[k] if k == 0 else spectra[k] + sign * spectra[k - 1]
         real, imag = spec[:block], spec[block:]
@@ -187,7 +190,7 @@
     inv_ref[:, 4 * block :] = high
 
 
-def call_filter(weights, skip, blocks, outs, block):
+def call_filter(weights, skip, after, blocks, block):
     w1, b1, w2, b2, w3, decay = weights
     length = blocks * block
     emb, order = w1.shape
@@ -199,16 +202,17 @@
         inverse.astype(np.float32), skip[None],
     ]
     out_shape = [
-        VMEM((blocks, block, LANES), F32),
-        VMEM((blocks, block, LANES), F32),
-        VMEM((blocks, 8, LANES), F32),
+        VMEM((blocks, block, WIDE), F32),
+        VMEM((blocks, block, WIDE), F32),
+        VMEM((blocks, 8, WIDE), F32),
         VMEM((2 * block, 2 * block), BF16),
         VMEM((block, 6 * block), BF16),
-        VMEM((1, LANES), F32),
+        VMEM((1, WIDE), F32),
     ]
     return pl.pallas_call(
-        functools.partial(filter_kernel, blocks, block, outs, pad),
-        in_specs=[pl.BlockSpec(memory_space=pltpu.HBM)] * len(hbm),
+        functools.partial(filter_kernel, blocks, block, pad),
+        in_specs=[pl.BlockSpec(memory_space=pltpu.HBM)] * len(hbm)
+        + [pl.BlockSpec(memory_space=pl.ANY)],
         out_specs=[pl.BlockSpec(memory_space=VMEM)] * len(out_shape),
         out_shape=out_shape,
         scratch_shapes=[
@@ -230,7 +234,11 @@
             flops=4 * 10**8, bytes_accessed=8 * 2**20, transcendentals=length * LANES
         ),
         name="filter_spectra",
-    )(*(pltpu.with_memory_space_constraint(jnp.asarray(each), pltpu.HBM) for each in hbm))
+    )(*(pltpu.with_memory_space_constraint(jnp.asarray(each), pltpu.HBM) for each in hbm), after)
+
+
+def lanes_of(core):
+    return pl.ds(pl.multiple_of(core * WIDE, LANES), WIDE)
 
 
 def columns_of(part, half, width):
@@ -255,20 +263,17 @@
     return copies
 
 
-def pack_kernel(blocks, outs, x_ref, gate_ref, weight_ref, pieces_ref, *refs):
-    gate_refs, (over_x_ref, over_y_ref, sems) = refs[:outs], refs[outs:]
-    group = lax.axis_index("seq") % outs
-    copies = [
-        pltpu.make_async_copy(
-            x_ref.at[:, (d % outs) * LANES : (d % outs + 1) * LANES], pieces_ref.at[d], sems.at[d]
-        )
-        for d in range(blocks)
-    ]
-    for k in range(outs):
-        lanes = pl.ds(pl.multiple_of((group ^ k) * LANES, LANES), LANES)
-        copies.append(
-            pltpu.make_async_copy(gate_ref.at[:, lanes], gate_refs[k], sems.at[len(copies)])
-        )
+def pack_kernel(x_ref, gate_ref, weight_ref, mine_ref, other_ref, over_x_ref, over_y_ref, sems):
+    block = x_ref.shape[0]
+    core = lax.axis_index("seq") % CORES
+    copies = []
+    for place, out_ref in ((1 - core, other_ref), (core, mine_ref)):
+        for source, rows in ((x_ref, slice(0, block)), (gate_ref, slice(block, 2 * block))):
+            copies.append(
+                pltpu.make_async_copy(
+                    source.at[:, lanes_of(place)], out_ref.at[rows], sems.at[len(copies)]
+                )
+            )
     copies += weight_copies(weight_ref, over_x_ref, over_y_ref, sems, len(copies))
     for copy in copies:
         copy.start()
@@ -276,58 +281,73 @@
         copy.wait()
 
 
-def call_pack(x, gate, weight, blocks, outs):
-    block = x.shape[0]
+def call_pack(x, gate, weight):
+    both = VMEM((2 * x.shape[0], WIDE), BF16)
     send = VMEM((weight.shape[0] // 2, weight.shape[1] // FACE), BF16)
-    out_shape = [jax.ShapeDtypeStruct((blocks, block, LANES), BF16)]
-    out_shape += [jax.ShapeDtypeStruct((block, LANES), BF16)] * outs + [send] * 2
     return pl.pallas_call(
-        functools.partial(pack_kernel, blocks, outs),
+        pack_kernel,
         in_specs=[pl.BlockSpec(memory_space=pltpu.HBM)] * 3,
-        out_specs=[pl.BlockSpec(memory_space=VMEM)] * len(out_shape),
-        out_shape=out_shape,
-        scratch_shapes=[pltpu.SemaphoreType.DMA((blocks + outs + 4,))],
+        out_specs=[pl.BlockSpec(memory_space=VMEM)] * 4,
+        out_shape=[both, both, send, send],
+        scratch_shapes=[pltpu.SemaphoreType.DMA((8,))],
         cost_estimate=pl.CostEstimate(flops=0, bytes_accessed=2**21, transcendentals=0),
         name="pack_pieces",
     )(*(pltpu.with_memory_space_constraint(each, pltpu.HBM) for each in (x, gate, weight)))
 
 
-def conv_kernel(blocks, outs, block, xs_ref, *refs):
-    gate_refs, refs = refs[:outs], refs[outs:]
+def order_kernel(mine_ref, theirs_ref, x_ref, gate_ref):
+    block = mine_ref.shape[0] // 2
+    core = lax.axis_index("seq") % CORES
+    for place, source in ((core, mine_ref), (1 - core, theirs_ref)):
+        rows = pl.ds(pl.multiple_of(place * block, LANES), block)
+        x_ref[rows] = source[:block]
+        gate_ref[rows] = source[block:]
+
+
+def conv_kernel(blocks, block, *refs):
+    source_refs, gate_ref, refs = refs[:CHIPS], refs[CHIPS], refs[CHIPS + 1 :]
     hre_ref, him_ref, hfirst_ref, fwd_ref, inv_ref, skip_ref = refs[:6]
-    refs = refs[8:]
-    out_refs, (wre_ref, wim_ref, yre_ref, yim_ref) = refs[:outs], refs[outs + 2 :]
+    keep_ref, send_ref = refs[8:10]
+    wre_ref, wim_ref, yre_ref, yim_ref = refs[12:]
     me = lax.axis_index("seq")
-    half, group = me // outs, me % outs
-    earlier = blocks - outs
-    for j in range(outs):
-        values = jnp.concatenate([xs_ref[j], xs_ref[half * outs + j]], axis=1)
-        spec = jnp.dot(
-            fwd_ref[...], jnp.concatenate([values, values], axis=0), preferred_element_type=F32
-        )
-        before = jnp.where(half > 0, spec[:, :LANES], 0.0)
-        wre_ref[j] = before[:block]
-        wim_ref[j] = before[block:]
-        wre_ref[earlier + j] = spec[:block, LANES:]
-        wim_ref[earlier + j] = spec[block:, LANES:]
+    core, chip = me % CORES, me // CORES
+    behind = [jnp.zeros((), jnp.int32)]
+    for k in range(CHIPS):
+        distance = chip - (chip ^ k)
+        if k:
+            behind.append(jnp.maximum(distance, 1) * CORES)
+        for b in range(CORES):
+            values = source_refs[k][b * block : (b + 1) * block]
+            spec = jnp.dot(
+                fwd_ref[...], jnp.concatenate([values, values], axis=0), preferred_element_type=F32
+            )
+            if k:
+                spec = jnp.where(distance > 0, spec, 0.0)
+            wre_ref[k * CORES + b] = spec[:block]
+            wim_ref[k * CORES + b] = spec[block:]
 
     def rows_at(start, first):
         rows = pl.ds(start, 8)
-        wre = [wre_ref[j, rows, :] for j in range(blocks)]
-        wim = [wim_ref[j, rows, :] for j in range(blocks)]
-        for o in range(outs):
-            total_re = total_im = None
-            for j in range(earlier + o + 1):
-                k = earlier + o - j
-                hre = hre_ref[k, rows, :]
-                him = him_ref[k, rows, :]
-                hother = hfirst_ref[k] if first else hre
-                add_re = wre[j] * hre - wim[j] * him
-                add_im = wre[j] * him + wim[j] * hother
-                total_re = add_re if total_re is None else total_re + add_re
-                total_im = add_im if total_im is None else total_im + add_im
-            yre_ref[o, rows, :] = total_re
-            yim_ref[o, rows, :] = total_im
+        for lanes in (slice(0, LANES), slice(LANES, WIDE)):
+            totals = [None] * (2 * CORES)
+            for k in range(CHIPS):
+                for b in range(CORES):
+                    wre = wre_ref[k * CORES + b, rows, lanes]
+                    wim = wim_ref[k * CORES + b, rows, lanes]
+                    for o in range(CORES):
+                        if k == 0 and o < b:
+                            continue
+                        lag = behind[k] + (o - b)
+                        hre = hre_ref[lag, rows, lanes]
+                        him = him_ref[lag, rows, lanes]
+                        hother = hfirst_ref[lag, :, lanes] if first else hre
+                        adds = (wre * hre - wim * him, wre * him + wim * hother)
+                        for i, add in enumerate(adds):
+                            old = totals[2 * o + i]
+                            totals[2 * o + i] = add if old is None else old + add
+            for o in range(CORES):
+                yre_ref[o, rows, lanes] = totals[2 * o]
+                yim_ref[o, rows, lanes] = totals[2 * o + 1]
 
     rows_at(0, True)
 
@@ -335,56 +355,47 @@
     def _(tile):
         rows_at(pl.multiple_of(tile * 8, 8), False)
 
-    def stacked(slot):
-        re_high, re_low = split_value(yre_ref[slot])
-        im_high, im_low = split_value(yim_ref[slot])
-        return jnp.concatenate([re_high, im_high, re_high, im_high, re_low, im_low], axis=0)
-
-    skip = skip_ref[...]
-    for k in range(0, outs, 2):
-        pair = jnp.concatenate([stacked(group ^ k), stacked(group ^ (k + 1))], axis=1)
-        conv = jnp.dot(inv_ref[...], pair, preferred_element_type=F32)
-        for i in range(2):
-            values = xs_ref[half * outs + (group ^ (k + i))].astype(F32)
-            gate = gate_refs[k + i][...].astype(F32)
-            mixed = conv[:, i * LANES : (i + 1) * LANES] + skip * values
-            out_refs[k + i][...] = (gate * mixed).astype(BF16)
-
-
-def call_conv(xs, gates, filters, passing):
-    blocks, block, _ = xs.shape
-    outs = len(gates)
+    for place, out_ref in ((1 - core, send_ref), (core, keep_ref)):
+        re_high, re_low = split_value(yre_ref[place])
+        im_high, im_low = split_value(yim_ref[place])
+        stacked = jnp.concatenate([re_high, im_high, re_high, im_high, re_low, im_low], axis=0)
+        conv = jnp.dot(inv_ref[...], stacked, preferred_element_type=F32)
+        rows = pl.ds(pl.multiple_of(place * block, LANES), block)
+        values = source_refs[0][rows].astype(F32)
+        gate = gate_ref[rows].astype(F32)
+        out_ref[...] = (gate * (conv + skip_ref[...] * values)).astype(BF16)
+
+
+def call_conv(sources, gate, filters, passing, blocks, block):
     pinned = [pltpu.with_memory_space_constraint(each, VMEM) for each in filters]
-    operands = [xs, *gates, *pinned]
+    operands = [*sources, gate, *pinned]
     shape = jax.ShapeDtypeStruct
     return pl.pallas_call(
-        functools.partial(conv_kernel, blocks, outs, block),
+        functools.partial(conv_kernel, blocks, block),
         in_specs=[pl.BlockSpec(memory_space=VMEM)] * len(operands)
         + [pl.BlockSpec(memory_space=pl.ANY)] * 2,
-        out_specs=[pl.BlockSpec(memory_space=VMEM)] * outs
+        out_specs=[pl.BlockSpec(memory_space=VMEM)] * 2
         + [pl.BlockSpec(memory_space=pl.ANY)] * 2,
-        out_shape=[shape((block, LANES), BF16)] * outs + [shape(p.shape, p.dtype) for p in passing],
-        input_output_aliases={len(operands) + i: outs + i for i in range(2)},
+        out_shape=[shape((block, WIDE), BF16)] * 2 + [shape(p.shape, p.dtype) for p in passing],
+        input_output_aliases={len(operands) + i: 2 + i for i in range(2)},
         scratch_shapes=[
-            VMEM((blocks, block, LANES), F32),
-            VMEM((blocks, block, LANES), F32),
-            VMEM((outs, block, LANES), F32),
-            VMEM((outs, block, LANES), F32),
+            VMEM((blocks, block, WIDE), F32),
+            VMEM((blocks, block, WIDE), F32),
+            VMEM((CORES, block, WIDE), F32),
+            VMEM((CORES, block, WIDE), F32),
         ],
         compiler_params=pltpu.CompilerParams(vmem_limit_bytes=16 * 2**20),
         cost_estimate=pl.CostEstimate(
-            flops=2 * 10**8, bytes_accessed=3 * 2**20, transcendentals=0
+            flops=3 * 10**8, bytes_accessed=3 * 2**20, transcendentals=0
         ),
         name="convolve",
     )(*operands, *passing)
 
 
-def join_kernel(outs, *refs):
-    piece_refs, joined_ref = refs[:outs], refs[outs]
-    group = lax.axis_index("seq") % outs
-    for k in range(outs):
-        lanes = pl.ds(pl.multiple_of((group ^ k) * LANES, LANES), LANES)
-        joined_ref[:, lanes] = piece_refs[k][...]
+def join_kernel(mine_ref, theirs_ref, joined_ref):
+    core = lax.axis_index("seq") % CORES
+    joined_ref[:, lanes_of(core)] = mine_ref[...]
+    joined_ref[:, lanes_of(1 - core)] = theirs_ref[...]
 
 
 def tiles(width):
@@ -486,34 +497,37 @@
 ):
     block, width = mixer_input.shape
     blocks = lax.axis_size("seq")
-    outs = width // LANES
-
-    along_seq = lambda part, k: lax.ppermute(part, "seq", [(s, s ^ k) for s in range(blocks)])
+    shape = jax.ShapeDtypeStruct
     along_chan = lambda part, k: lax.ppermute(part, "chan", [(c, c ^ k) for c in range(FACE)])
-    to_partners = lambda parts: [parts[0]] + [along_seq(parts[k], k) for k in range(1, outs)]
-
-    xs, *gates, over_x, over_y = call_pack(
-        mixer_input, gate_branch, output_weight, blocks, outs
-    )
-    xs = lax.all_to_all(xs, "seq", 0, 0, tiled=True)
+
+    def along_seq(part, k, senders=range(blocks)):
+        return lax.ppermute(part, "seq", [(s, s ^ k) for s in senders])
+
+    mine, other, over_x, over_y = call_pack(mixer_input, gate_branch, output_weight)
     from_x, from_y = along_chan(over_x, 1), along_chan(over_y, 2)
+    x, gate = in_vmem(
+        order_kernel,
+        [mine, along_seq(other, 1)],
+        [shape((2 * block, WIDE), BF16)] * 2,
+        "order_tokens",
+        10**6,
+    )
+    far = along_seq(x, 4, [s for s in range(blocks) if s // 4 == 0])
+    near = along_seq(x, 2, [s for s in range(blocks) if s // 2 % 2 == 0])
+    passed = along_seq(far, 2, [s for s in range(blocks) if s // 4 == 1])
     filters = call_filter(
         (first_weight, first_bias, second_weight, second_bias, last_weight, decay_rate),
         skip_gain,
+        x,
         blocks,
-        outs,
         block,
     )
-    *pieces, from_x, from_y = call_conv(xs, to_partners(gates), filters, (from_x, from_y))
+    keep, send, from_x, from_y = call_conv(
+        [x, near, far, passed], gate, filters, (from_x, from_y), blocks, block
+    )
     from_x, from_y = (from_x, along_seq(from_x, 1)), (from_y, along_seq(from_y, 1))
-    pieces = to_partners(pieces)
-    shape = jax.ShapeDtypeStruct
     gated = in_vmem(
-        functools.partial(join_kernel, outs),
-        pieces,
-        shape((block, width), BF16),
-        "join_pieces",
-        10**6,
+        join_kernel, [keep, along_seq(send, 1)], shape((block, width), BF16), "join_channels", 10**6
     )
     x_gated, y_gated = along_chan(gated, 1), along_chan(gated, 2)
     send_a, send_b, keep_a, keep_b = call_own(gated, output_weight)
@@ -648,12 +662,10 @@
 
     def shards(mixer_input, *rest):
         block, width = mixer_input.shape
-        outs = width // LANES
         splits = (
-            width % LANES == 0
+            width == CORES * WIDE
             and block % LANES == 0
-            and seq_count == 2 * outs
-            and outs == 4
+            and seq_count == CORES * CHIPS
             and chan_count == FACE
         )
         plan = split_shards if splits else gathered_shards

time: 42.4 us -> 42.3 us (level)
  the two profiles are of different devices: /device:TPU:0 before, /device:TPU:24 now
where the time goes in v1:
time: 42.3 us; the launch traced here: 42.1 us
  waiting for transfers between devices  21.1 us (50%)
  starting transfers between devices  11.4 us (27%)
  Pallas kernels  9.41 us (22%)
    ppermute x7, waiting for transfers between devices, along_seq(): return lax.ppermute(part, 'seq', [(s, s ^ k) for s in senders])  14.3 us
    ppermute x6, waiting for transfers between devices, split_shards(): lax.ppermute(part, 'chan', [(c, c ^ k) for c in range(FACE)])  6.82 us
    ppermute x6, starting transfers between devices, split_shards(): lax.ppermute(part, 'chan', [(c, c ^ k) for c in range(FACE)])  6.3 us
    ppermute x7, starting transfers between devices, along_seq(): return lax.ppermute(part, 'seq', [(s, s ^ k) for s in senders])  5.14 us
    pallas_call x1, Pallas kernels, call_filter(): pl.pallas_call(functools.partial(filter_kernel, blocks, block, pad), in_s...  3.11 us
    pallas_call x1, Pallas kernels, call_own(): pl.pallas_call(functools.partial(own_kernel, columns), in_specs=[pl.Block...  2.02 us
    pallas_call x1, Pallas kernels, call_conv(): pl.pallas_call(functools.partial(conv_kernel, blocks, block), in_specs=[p...  1.46 us
    pallas_call x5, Pallas kernels, in_vmem(): pl.pallas_call(kernel, in_specs=[pl.BlockSpec(memory_space=VMEM)] * len(o...  1.42 us
  transfers between devices with their start and end apart: 13, of which 8 were waited for; matrix products, arithmetic and copies ran while one was open for 0% of the time, Pallas kernels for 13%

profile of v1, /device:TPU:24, one launch (start us, length us, event | category | flops | bytes accessed | tf_op | source)
XLA Modules:
  0.0 42.1 jit_solution(15275026529037855848)
XLA Ops:
  0.0 1.4 %pack_pieces.1 = (bf16[256,256]{1,0:T(8,128)(2,1)S(1)}, bf16[256,256]{1,0:T(8,128)(2,1)S(1)}, bf16[256,1024]{1,0:T(8,128)(2,1)S(1)}, bf16[256,1024]{1,0:T(8,128)(2,1)S(1)}) custom-call(bf16[128,512]{1,0:T(8,128)(2,1)} %x_ref.1, bf16[128,512]{1,0:T(8,128)(2,1)} %gate_ref.1, bf16[512,4096]{1,0:T(8,128)(2,1)} %weight_ref.3), custom_call_target="tpu_custom_call" | custom-call | bytes 2097152 | tf_op jit(solution)/shard_map/pack_pieces/pallas_call | solution.py:287
  1.4 1.6 %collective-permute-start.4 = (bf16[256,1024]{1,0:T(8,128)(2,1)S(1)}, bf16[256,1024]{1,0:T(8,128)(2,1)S(1)}, u32[]{:S(2)}, u32[]{:S(2)}) collective-permute-start(bf16[256,1024]{1,0:T(8,128)(2,1)S(1)} %get-tuple-element.39), channel_id=1, source_target_pairs={{0,1},{1,0},{2,3},{3,2},{4,5},{5,4},{6,7},{7,6},{8,9},{9,8},{10,11... | collective-permute-start | bytes 1572872 | tf_op jit(solution)/shard_map/ppermute | solution.py:501
  3.0 1.5 %collective-permute-start.5 = (bf16[256,1024]{1,0:T(8,128)(2,1)S(1)}, bf16[256,1024]{1,0:T(8,128)(2,1)S(1)}, u32[]{:S(2)}, u32[]{:S(2)}) collective-permute-start(bf16[256,1024]{1,0:T(8,128)(2,1)S(1)} %get-tuple-element.40), channel_id=1, source_target_pairs={{0,2},{1,3},{2,0},{3,1},{4,6},{5,7},{6,4},{7,5},{8,10},{9,11},{10,... | collective-permute-start | bytes 1572872 | tf_op jit(solution)/shard_map/ppermute | solution.py:501
  4.5 0.0 collective-permute-start
  4.5 1.3 %collective-permute-done.theirs_ref = bf16[256,256]{1,0:T(8,128)(2,1)S(1)} collective-permute-done((bf16[256,256]{1,0:T(8,128)(2,1)S(1)}, bf16[256,256]{1,0:T(8,128)(2,1)S(1)}, u32[]{:S(2)}, u32[]{:S(2)}) %collective-permute-start) | collective-permute-done | bytes 131104 | tf_op jit(solution)/shard_map/ppermute | solution.py:504
  5.9 1.3 %collective-permute-start.2 = (bf16[256,256]{1,0:T(8,128)(2,1)S(1)}, bf16[256,256]{1,0:T(8,128)(2,1)S(1)}, u32[]{:S(2)}, u32[]{:S(2)}) collective-permute-start(bf16[256,256]{1,0:T(8,128)(2,1)S(1)} %get-tuple-element.31.refs_10_.refs_0_), channel_id=1, source_target_pairs={{0,16},{4,20},{8,24},{12,28},{1,17},{5,21},{9,25},{13,29},{2,18},{... | collective-permute-start | bytes 393224 | tf_op jit(solution)/shard_map/ppermute | solution.py:504
  7.2 1.3 %collective-permute-start.1 = (bf16[256,256]{1,0:T(8,128)(2,1)S(1)}, bf16[256,256]{1,0:T(8,128)(2,1)S(1)}, u32[]{:S(2)}, u32[]{:S(2)}) collective-permute-start(bf16[256,256]{1,0:T(8,128)(2,1)S(1)} %get-tuple-element.31.refs_10_.refs_0_), channel_id=1, source_target_pairs={{0,8},{4,12},{16,24},{20,28},{1,9},{5,13},{17,25},{21,29},{2,10},{... | collective-permute-start | bytes 393224 | tf_op jit(solution)/shard_map/ppermute | solution.py:504
  8.5 8.5 %collective-permute-done.2.refs_2_ = bf16[256,256]{1,0:T(8,128)(2,1)S(1)} collective-permute-done((bf16[256,256]{1,0:T(8,128)(2,1)S(1)}, bf16[256,256]{1,0:T(8,128)(2,1)S(1)}, u32[]{:S(2)}, u32[]{:S(2)}) %collective-permute-start.2) | collective-permute-done | bytes 131104 | tf_op jit(solution)/shard_map/ppermute | solution.py:504
  17.0 1.9 %collective-permute-start.3 = (bf16[256,256]{1,0:T(8,128)(2,1)S(1)}, bf16[256,256]{1,0:T(8,128)(2,1)S(1)}, u32[]{:S(2)}, u32[]{:S(2)}) collective-permute-start(bf16[256,256]{1,0:T(8,128)(2,1)S(1)} %collective-permute-done.2.refs_2_), channel_id=1, source_target_pairs={{16,24},{20,28},{24,16},{28,20},{17,25},{21,29},{25,17},{29,21},{1... | collective-permute-start | bytes 393224 | tf_op jit(solution)/shard_map/ppermute | solution.py:504
  18.9 3.1 %filter_spectra.1 = (f32[8,128,256]{2,1,0:T(8,128)S(1)}, f32[8,128,256]{2,1,0:T(8,128)S(1)}, f32[8,8,256]{2,1,0:T(8,128)S(1)}, bf16[256,256]{1,0:T(8,128)(2,1)S(...) custom-call(f32[33,64]{1,0:T(8,128)} %refs_0_.1, f32[512,240]{1,0:T(8,128)} %constant.6.clone.refs_1_, ...), custom_call_target="tpu_custom_call" | custom-call | flops 400000000 | bytes 8388608 | tf_op jit(solution)/shard_map/filter_spectra/pallas_call | solution.py:212
  22.1 0.0 collective-permute-done.1.refs_1_
  22.1 2.2 %collective-permute-done.3.refs_3_ = bf16[256,256]{1,0:T(8,128)(2,1)S(1)} collective-permute-done((bf16[256,256]{1,0:T(8,128)(2,1)S(1)}, bf16[256,256]{1,0:T(8,128)(2,1)S(1)}, u32[]{:S(2)}, u32[]{:S(2)}) %collective-permute-start.3) | collective-permute-done | bytes 131104 | tf_op jit(solution)/shard_map/ppermute | solution.py:504
  24.3 0.0 collective-permute-done.4.refs_11_
  24.3 0.0 collective-permute-done.5.refs_12_
  24.3 1.5 %convolve.1 = (bf16[128,256]{1,0:T(8,128)(2,1)S(1)}, bf16[128,256]{1,0:T(8,128)(2,1)S(1)}, bf16[256,1024]{1,0:T(8,128)(2,1)S(1)}, bf16[256,1024]{1,0:T(8,128)(2,1)S(1)}) custom-call(bf16[256,256]{1,0:T(8,128)(2,1)S(1)} %get-tuple-element.31.refs_10_.refs_0_, ...), custom_call_target="tpu_custom_call", output_to_operand_aliasing={{2}: (11, {}), {3}: (12, {})} | custom-call | flops 300000000 | bytes 3145728 | tf_op jit(solution)/shard_map/convolve/pallas_call | solution.py:373
  25.8 0.1 collective-permute-start.9
  25.8 0.5 %collective-permute-start.10 = (bf16[256,1024]{1,0:T(8,128)(2,1)S(1)}, bf16[256,1024]{1,0:T(8,128)(2,1)S(1)}, u32[]{:S(2)}, u32[]{:S(2)}) collective-permute-start(bf16[256,1024]{1,0:T(8,128)(2,1)S(1)} %get-tuple-element.44.refs_2_), channel_id=1, source_target_pairs={{0,4},{4,0},{8,12},{12,8},{16,20},{20,16},{24,28},{28,24},{1,5},{5... | collective-permute-start | bytes 1572872 | tf_op jit(solution)/shard_map/ppermute | solution.py:504
  26.3 0.1 collective-permute-start.6
  26.4 2.2 %collective-permute-done.6.theirs_ref = bf16[128,256]{1,0:T(8,128)(2,1)S(1)} collective-permute-done((bf16[128,256]{1,0:T(8,128)(2,1)S(1)}, bf16[128,256]{1,0:T(8,128)(2,1)S(1)}, u32[]{:S(2)}, u32[]{:S(2)}) %collective-permute-start.6) | collective-permute-done | bytes 65568 | tf_op jit(solution)/shard_map/ppermute | solution.py:504
  28.6 0.6 %collective-permute-start.8 = (bf16[128,512]{1,0:T(8,128)(2,1)S(1)}, bf16[128,512]{1,0:T(8,128)(2,1)S(1)}, u32[]{:S(2)}, u32[]{:S(2)}) collective-permute-start(bf16[128,512]{1,0:T(8,128)(2,1)S(1)} %join_channels.1.gated_ref), channel_id=1, source_target_pairs={{0,2},{1,3},{2,0},{3,1},{4,6},{5,7},{6,4},{7,5},{8,10},{9,11},{10,... | collective-permute-start | bytes 393224 | tf_op jit(solution)/shard_map/ppermute | solution.py:501
  29.2 0.5 %collective-permute-start.7 = (bf16[128,512]{1,0:T(8,128)(2,1)S(1)}, bf16[128,512]{1,0:T(8,128)(2,1)S(1)}, u32[]{:S(2)}, u32[]{:S(2)}) collective-permute-start(bf16[128,512]{1,0:T(8,128)(2,1)S(1)} %join_channels.1.gated_ref), channel_id=1, source_target_pairs={{0,1},{1,0},{2,3},{3,2},{4,5},{5,4},{6,7},{7,6},{8,9},{9,8},{10,11... | collective-permute-start | bytes 393224 | tf_op jit(solution)/shard_map/ppermute | solution.py:501
  29.7 2.0 %own_channels.1 = (f32[128,512]{1,0:T(8,128)S(1)}, f32[128,512]{1,0:T(8,128)S(1)}, f32[128,512]{1,0:T(8,128)S(1)}, f32[128,512]{1,0:T(8,128)S(1)}) custom-call(bf16[128,512]{1,0:T(8,128)(2,1)S(1)} %join_channels.1.gated_ref, bf16[512,4096]{1,0:T(8,128)(2,1)} %weight_ref.3), custom_call_target="tpu_custom_call" | custom-call | flops 268435456 | bytes 3145728 | tf_op jit(solution)/shard_map/own_channels/pallas_call | solution.py:469
  31.7 2.5 %collective-permute-done.8.y_ref = bf16[128,512]{1,0:T(8,128)(2,1)S(1)} collective-permute-done((bf16[128,512]{1,0:T(8,128)(2,1)S(1)}, bf16[128,512]{1,0:T(8,128)(2,1)S(1)}, u32[]{:S(2)}, u32[]{:S(2)}) %collective-permute-start.8) | collective-permute-done | bytes 131104 | tf_op jit(solution)/shard_map/ppermute | solution.py:501
  34.2 0.2 collective-permute-done.7.x_ref
  34.4 0.0 collective-permute-done.9.refs_1_
  34.4 0.0 collective-permute-done.10.refs_3_
  34.4 0.3 sums_to_send.1
  34.8 1.6 %collective-permute-start.11 = (bf16[128,512]{1,0:T(8,128)(2,1)S(1)}, bf16[128,512]{1,0:T(8,128)(2,1)S(1)}, u32[]{:S(2)}, u32[]{:S(2)}) collective-permute-start(bf16[128,512]{1,0:T(8,128)(2,1)S(1)} %get-tuple-element.51), channel_id=1, source_target_pairs={{0,2},{1,3},{2,0},{3,1},{4,6},{5,7},{6,4},{7,5},{8,10},{9,11},{10,... | collective-permute-start | bytes 393224 | tf_op jit(solution)/shard_map/ppermute | solution.py:501
  36.3 0.5 %collective-permute-start.12 = (bf16[128,512]{1,0:T(8,128)(2,1)S(1)}, bf16[128,512]{1,0:T(8,128)(2,1)S(1)}, u32[]{:S(2)}, u32[]{:S(2)}) collective-permute-start(bf16[128,512]{1,0:T(8,128)(2,1)S(1)} %get-tuple-element.52), channel_id=1, source_target_pairs={{0,1},{1,0},{2,3},{3,2},{4,5},{5,4},{6,7},{7,6},{8,9},{9,8},{10,11... | collective-permute-start | bytes 393224 | tf_op jit(solution)/shard_map/ppermute | solution.py:501
  36.9 0.3 sums_to_keep.1
  37.2 2.6 %collective-permute-done.11.refs_2_ = bf16[128,512]{1,0:T(8,128)(2,1)S(1)} collective-permute-done((bf16[128,512]{1,0:T(8,128)(2,1)S(1)}, bf16[128,512]{1,0:T(8,128)(2,1)S(1)}, u32[]{:S(2)}, u32[]{:S(2)}) %collective-permute-start.11) | collective-permute-done | bytes 131104 | tf_op jit(solution)/shard_map/ppermute | solution.py:501
  39.8 1.5 %collective-permute-done.12.refs_3_ = bf16[128,512]{1,0:T(8,128)(2,1)S(1)} collective-permute-done((bf16[128,512]{1,0:T(8,128)(2,1)S(1)}, bf16[128,512]{1,0:T(8,128)(2,1)S(1)}, u32[]{:S(2)}, u32[]{:S(2)}) %collective-permute-start.12) | collective-permute-done | bytes 131104 | tf_op jit(solution)/shard_map/ppermute | solution.py:501
  41.3 0.7 %last_sum.1 = bf16[128,1024]{1,0:T(8,128)(2,1)} custom-call(f32[128,512]{1,0:T(8,128)S(1)} %get-tuple-element.47.refs_0_, f32[128,512]{1,0:T(8,128)S(1)} %get-tuple-element.48.refs_1_, bf16[128,512]{1,0:T(8,128)(2,1)S(1)} %collective-permute-done.11.refs_2_, bf16[128,512]{1,0:T(8,128)(2,1)S(1)} %collective-permute-done.12.refs_3_), custom_call_target="tpu_custom_call" | custom-call | flops 1000000 | bytes 1048576 | tf_op jit(solution)/shard_map/last_sum/pallas_call | solution.py:454
  (2 shorter events, 0.1 us)
Async XLA Ops:
  1.4 22.9 %collective-permute-start.4 = (bf16[256,1024]{1,0:T(8,128)(2,1)S(1)}, bf16[256,1024]{1,0:T(8,128)(2,1)S(1)}, u32[]{:S(2)}, u32[]{:S(2)}) collective-permute-start(bf16[256,1024]{1,0:T(8,128)(2,1)S(1)} %get-tuple-element.39), channel_id=1, source_target_pairs={{0,1},{1,0},{2,3},{3,2},{4,5},{5,4},{6,7},{7,6},{8,9},{9,8},{10,11... | collective-permute-start | bytes 1572872 | tf_op jit(solution)/shard_map/ppermute | solution.py:501
  3.0 21.3 %collective-permute-start.5 = (bf16[256,1024]{1,0:T(8,128)(2,1)S(1)}, bf16[256,1024]{1,0:T(8,128)(2,1)S(1)}, u32[]{:S(2)}, u32[]{:S(2)}) collective-permute-start(bf16[256,1024]{1,0:T(8,128)(2,1)S(1)} %get-tuple-element.40), channel_id=1, source_target_pairs={{0,2},{1,3},{2,0},{3,1},{4,6},{5,7},{6,4},{7,5},{8,10},{9,11},{10,... | collective-permute-start | bytes 1572872 | tf_op jit(solution)/shard_map/ppermute | solution.py:501
  4.5 1.3 %collective-permute-start = (bf16[256,256]{1,0:T(8,128)(2,1)S(1)}, bf16[256,256]{1,0:T(8,128)(2,1)S(1)}, u32[]{:S(2)}, u32[]{:S(2)}) collective-permute-start(bf16[256,256]{1,0:T(8,128)(2,1)S(1)} %get-tuple-element.30), channel_id=1, source_target_pairs={{0,4},{4,0},{8,12},{12,8},{16,20},{20,16},{24,28},{28,24},{1,5},{5... | collective-permute-start | bytes 393224 | tf_op jit(solution)/shard_map/ppermute | solution.py:504
  5.9 11.1 %collective-permute-start.2 = (bf16[256,256]{1,0:T(8,128)(2,1)S(1)}, bf16[256,256]{1,0:T(8,128)(2,1)S(1)}, u32[]{:S(2)}, u32[]{:S(2)}) collective-permute-start(bf16[256,256]{1,0:T(8,128)(2,1)S(1)} %get-tuple-element.31.refs_10_.refs_0_), channel_id=1, source_target_pairs={{0,16},{4,20},{8,24},{12,28},{1,17},{5,21},{9,25},{13,29},{2,18},{... | collective-permute-start | bytes 393224 | tf_op jit(solution)/shard_map/ppermute | solution.py:504
  7.2 14.9 %collective-permute-start.1 = (bf16[256,256]{1,0:T(8,128)(2,1)S(1)}, bf16[256,256]{1,0:T(8,128)(2,1)S(1)}, u32[]{:S(2)}, u32[]{:S(2)}) collective-permute-start(bf16[256,256]{1,0:T(8,128)(2,1)S(1)} %get-tuple-element.31.refs_10_.refs_0_), channel_id=1, source_target_pairs={{0,8},{4,12},{16,24},{20,28},{1,9},{5,13},{17,25},{21,29},{2,10},{... | collective-permute-start | bytes 393224 | tf_op jit(solution)/shard_map/ppermute | solution.py:504
  17.0 7.3 %collective-permute-start.3 = (bf16[256,256]{1,0:T(8,128)(2,1)S(1)}, bf16[256,256]{1,0:T(8,128)(2,1)S(1)}, u32[]{:S(2)}, u32[]{:S(2)}) collective-permute-start(bf16[256,256]{1,0:T(8,128)(2,1)S(1)} %collective-permute-done.2.refs_2_), channel_id=1, source_target_pairs={{16,24},{20,28},{24,16},{28,20},{17,25},{21,29},{25,17},{29,21},{1... | collective-permute-start | bytes 393224 | tf_op jit(solution)/shard_map/ppermute | solution.py:504
  25.8 8.7 %collective-permute-start.9 = (bf16[256,1024]{1,0:T(8,128)(2,1)S(1)}, bf16[256,1024]{1,0:T(8,128)(2,1)S(1)}, u32[]{:S(2)}, u32[]{:S(2)}) collective-permute-start(bf16[256,1024]{1,0:T(8,128)(2,1)S(1)} %get-tuple-element.43.refs_0_), channel_id=1, source_target_pairs={{0,4},{4,0},{8,12},{12,8},{16,20},{20,16},{24,28},{28,24},{1,5},{5... | collective-permute-start | bytes 1572872 | tf_op jit(solution)/shard_map/ppermute | solution.py:504
  25.8 8.6 %collective-permute-start.10 = (bf16[256,1024]{1,0:T(8,128)(2,1)S(1)}, bf16[256,1024]{1,0:T(8,128)(2,1)S(1)}, u32[]{:S(2)}, u32[]{:S(2)}) collective-permute-start(bf16[256,1024]{1,0:T(8,128)(2,1)S(1)} %get-tuple-element.44.refs_2_), channel_id=1, source_target_pairs={{0,4},{4,0},{8,12},{12,8},{16,20},{20,16},{24,28},{28,24},{1,5},{5... | collective-permute-start | bytes 1572872 | tf_op jit(solution)/shard_map/ppermute | solution.py:504
  26.3 2.2 %collective-permute-start.6 = (bf16[128,256]{1,0:T(8,128)(2,1)S(1)}, bf16[128,256]{1,0:T(8,128)(2,1)S(1)}, u32[]{:S(2)}, u32[]{:S(2)}) collective-permute-start(bf16[128,256]{1,0:T(8,128)(2,1)S(1)} %get-tuple-element.42), channel_id=1, source_target_pairs={{0,4},{4,0},{8,12},{12,8},{16,20},{20,16},{24,28},{28,24},{1,5},{5... | collective-permute-start | bytes 196616 | tf_op jit(solution)/shard_map/ppermute | solution.py:504
  28.6 5.6 %collective-permute-start.8 = (bf16[128,512]{1,0:T(8,128)(2,1)S(1)}, bf16[128,512]{1,0:T(8,128)(2,1)S(1)}, u32[]{:S(2)}, u32[]{:S(2)}) collective-permute-start(bf16[128,512]{1,0:T(8,128)(2,1)S(1)} %join_channels.1.gated_ref), channel_id=1, source_target_pairs={{0,2},{1,3},{2,0},{3,1},{4,6},{5,7},{6,4},{7,5},{8,10},{9,11},{10,... | collective-permute-start | bytes 393224 | tf_op jit(solution)/shard_map/ppermute | solution.py:501
  29.2 5.3 %collective-permute-start.7 = (bf16[128,512]{1,0:T(8,128)(2,1)S(1)}, bf16[128,512]{1,0:T(8,128)(2,1)S(1)}, u32[]{:S(2)}, u32[]{:S(2)}) collective-permute-start(bf16[128,512]{1,0:T(8,128)(2,1)S(1)} %join_channels.1.gated_ref), channel_id=1, source_target_pairs={{0,1},{1,0},{2,3},{3,2},{4,5},{5,4},{6,7},{7,6},{8,9},{9,8},{10,11... | collective-permute-start | bytes 393224 | tf_op jit(solution)/shard_map/ppermute | solution.py:501
  34.8 5.0 %collective-permute-start.11 = (bf16[128,512]{1,0:T(8,128)(2,1)S(1)}, bf16[128,512]{1,0:T(8,128)(2,1)S(1)}, u32[]{:S(2)}, u32[]{:S(2)}) collective-permute-start(bf16[128,512]{1,0:T(8,128)(2,1)S(1)} %get-tuple-element.51), channel_id=1, source_target_pairs={{0,2},{1,3},{2,0},{3,1},{4,6},{5,7},{6,4},{7,5},{8,10},{9,11},{10,... | collective-permute-start | bytes 393224 | tf_op jit(solution)/shard_map/ppermute | solution.py:501
  36.3 5.0 %collective-permute-start.12 = (bf16[128,512]{1,0:T(8,128)(2,1)S(1)}, bf16[128,512]{1,0:T(8,128)(2,1)S(1)}, u32[]{:S(2)}, u32[]{:S(2)}) collective-permute-start(bf16[128,512]{1,0:T(8,128)(2,1)S(1)} %get-tuple-element.52), channel_id=1, source_target_pairs={{0,1},{1,0},{2,3},{3,2},{4,5},{5,4},{6,7},{7,6},{8,9},{9,8},{10,11... | collective-permute-start | bytes 393224 | tf_op jit(solution)/shard_map/ppermute | solution.py:501

commit v2 on v1

--- a/solution.py
+++ b/solution.py
@@ -305,7 +305,7 @@
 
 
 def conv_kernel(blocks, block, *refs):
-    source_refs, gate_ref, refs = refs[:CHIPS], refs[CHIPS], refs[CHIPS + 1 :]
+    x_ref, tokens_ref, gate_ref, refs = refs[0], refs[1], refs[2], refs[3:]
     hre_ref, him_ref, hfirst_ref, fwd_ref, inv_ref, skip_ref = refs[:6]
     keep_ref, send_ref = refs[8:10]
     wre_ref, wim_ref, yre_ref, yim_ref = refs[12:]
@@ -317,7 +317,8 @@
         if k:
             behind.append(jnp.maximum(distance, 1) * CORES)
         for b in range(CORES):
-            values = source_refs[k][b * block : (b + 1) * block]
+            rows = slice(b * block, (b + 1) * block)
+            values = tokens_ref[chip ^ k, rows] if k else x_ref[rows]
             spec = jnp.dot(
                 fwd_ref[...], jnp.concatenate([values, values], axis=0), preferred_element_type=F32
             )
@@ -361,14 +362,14 @@
         stacked = jnp.concatenate([re_high, im_high, re_high, im_high, re_low, im_low], axis=0)
         conv = jnp.dot(inv_ref[...], stacked, preferred_element_type=F32)
         rows = pl.ds(pl.multiple_of(place * block, LANES), block)
-        values = source_refs[0][rows].astype(F32)
+        values = x_ref[rows].astype(F32)
         gate = gate_ref[rows].astype(F32)
         out_ref[...] = (gate * (conv + skip_ref[...] * values)).astype(BF16)
 
 
-def call_conv(sources, gate, filters, passing, blocks, block):
+def call_conv(x, tokens, gate, filters, passing, blocks, block):
     pinned = [pltpu.with_memory_space_constraint(each, VMEM) for each in filters]
-    operands = [*sources, gate, *pinned]
+    operands = [x, tokens, gate, *pinned]
     shape = jax.ShapeDtypeStruct
     return pl.pallas_call(
         functools.partial(conv_kernel, blocks, block),
@@ -512,9 +513,8 @@
         "order_tokens",
         10**6,
     )
-    far = along_seq(x, 4, [s for s in range(blocks) if s // 4 == 0])
-    near = along_seq(x, 2, [s for s in range(blocks) if s // 2 % 2 == 0])
-    passed = along_seq(far, 2, [s for s in range(blocks) if s // 4 == 1])
+    same_core = [list(range(core, blocks, CORES)) for core in range(CORES)]
+    tokens = lax.all_gather(x, "seq", axis_index_groups=same_core)
     filters = call_filter(
         (first_weight, first_bias, second_weight, second_bias, last_weight, decay_rate),
         skip_gain,
@@ -523,7 +523,7 @@
         block,
     )
     keep, send, from_x, from_y = call_conv(
-        [x, near, far, passed], gate, filters, (from_x, from_y), blocks, block
+        x, tokens, gate, filters, (from_x, from_y), blocks, block
     )
     from_x, from_y = (from_x, along_seq(from_x, 1)), (from_y, along_seq(from_y, 1))
     gated = in_vmem(

time: 42.3 us -> 44.6 us (1.054)
  the two profiles are of different devices: /device:TPU:24 before, /device:TPU:0 now
where the time goes in v2:
time: 44.6 us; the launch traced here: 44.4 us
  blocking collectives  16.2 us (36%)
  waiting for transfers between devices  10.3 us (23%)
  Pallas kernels  9.41 us (21%)
  starting transfers between devices  8.39 us (19%)
    all_gather x1, blocking collectives, split_shards(): tokens = lax.all_gather(x, 'seq', axis_index_groups=same_core)  16.2 us
    ppermute x6, starting transfers between devices, split_shards(): lax.ppermute(part, 'chan', [(c, c ^ k) for c in range(FACE)])  7.74 us
    ppermute x6, waiting for transfers between devices, split_shards(): lax.ppermute(part, 'chan', [(c, c ^ k) for c in range(FACE)])  6.82 us
    ppermute x4, waiting for transfers between devices, along_seq(): return lax.ppermute(part, 'seq', [(s, s ^ k) for s in senders])  3.51 us
    pallas_call x1, Pallas kernels, call_filter(): pl.pallas_call(functools.partial(filter_kernel, blocks, block, pad), in_s...  3.11 us
    pallas_call x1, Pallas kernels, call_own(): pl.pallas_call(functools.partial(own_kernel, columns), in_specs=[pl.Block...  2.02 us
    pallas_call x1, Pallas kernels, call_conv(): pl.pallas_call(functools.partial(conv_kernel, blocks, block), in_specs=[p...  1.45 us
    pallas_call x5, Pallas kernels, in_vmem(): pl.pallas_call(kernel, in_specs=[pl.BlockSpec(memory_space=VMEM)] * len(o...  1.43 us
  transfers between devices with their start and end apart: 10, of which 6 were waited for; matrix products, arithmetic and copies ran while one was open for 0% of the time, Pallas kernels for 12%

profile of v2, /device:TPU:0, one launch (start us, length us, event | category | flops | bytes accessed | tf_op | source)
XLA Modules:
  0.0 44.4 jit_solution(17663394321147124930)
XLA Ops:
  0.0 1.4 %pack_pieces.1 = (bf16[256,256]{1,0:T(8,128)(2,1)S(1)}, bf16[256,256]{1,0:T(8,128)(2,1)S(1)}, bf16[256,1024]{1,0:T(8,128)(2,1)S(1)}, bf16[256,1024]{1,0:T(8,128)(2,1)S(1)}) custom-call(bf16[128,512]{1,0:T(8,128)(2,1)} %x_ref.1, bf16[128,512]{1,0:T(8,128)(2,1)} %gate_ref.1, bf16[512,4096]{1,0:T(8,128)(2,1)} %weight_ref.3), custom_call_target="tpu_custom_call" | custom-call | bytes 2097152 | tf_op jit(solution)/shard_map/pack_pieces/pallas_call | solution.py:287
  1.4 3.0 %collective-permute-start.1 = (bf16[256,1024]{1,0:T(8,128)(2,1)S(1)}, bf16[256,1024]{1,0:T(8,128)(2,1)S(1)}, u32[]{:S(2)}, u32[]{:S(2)}) collective-permute-start(bf16[256,1024]{1,0:T(8,128)(2,1)S(1)} %get-tuple-element.39), channel_id=1, source_target_pairs={{0,1},{1,0},{2,3},{3,2},{4,5},{5,4},{6,7},{7,6},{8,9},{9,8},{10,11... | collective-permute-start | bytes 1572872 | tf_op jit(solution)/shard_map/ppermute | solution.py:502
  4.4 1.5 %collective-permute-start.2 = (bf16[256,1024]{1,0:T(8,128)(2,1)S(1)}, bf16[256,1024]{1,0:T(8,128)(2,1)S(1)}, u32[]{:S(2)}, u32[]{:S(2)}) collective-permute-start(bf16[256,1024]{1,0:T(8,128)(2,1)S(1)} %get-tuple-element.40), channel_id=1, source_target_pairs={{0,2},{1,3},{2,0},{3,1},{4,6},{5,7},{6,4},{7,5},{8,10},{9,11},{10,... | collective-permute-start | bytes 1572872 | tf_op jit(solution)/shard_map/ppermute | solution.py:502
  5.9 0.0 collective-permute-start
  5.9 1.3 %collective-permute-done.theirs_ref = bf16[256,256]{1,0:T(8,128)(2,1)S(1)} collective-permute-done((bf16[256,256]{1,0:T(8,128)(2,1)S(1)}, bf16[256,256]{1,0:T(8,128)(2,1)S(1)}, u32[]{:S(2)}, u32[]{:S(2)}) %collective-permute-start) | collective-permute-done | bytes 131104 | tf_op jit(solution)/shard_map/ppermute | solution.py:505
  7.3 3.1 %filter_spectra.1 = (f32[8,128,256]{2,1,0:T(8,128)S(1)}, f32[8,128,256]{2,1,0:T(8,128)S(1)}, f32[8,8,256]{2,1,0:T(8,128)S(1)}, bf16[256,256]{1,0:T(8,128)(2,1)S(...) custom-call(f32[33,64]{1,0:T(8,128)} %refs_0_.1, f32[512,240]{1,0:T(8,128)} %constant.6.clone.refs_1_, ...), custom_call_target="tpu_custom_call" | custom-call | flops 400000000 | bytes 8388608 | tf_op jit(solution)/shard_map/filter_spectra/pallas_call | solution.py:212
  10.4 16.2 %all-gather = bf16[1024,256]{1,0:T(8,128)(2,1)S(1)} all-gather(bf16[256,256]{1,0:T(8,128)(2,1)S(1)} %get-tuple-element.31.refs_10_.refs_0_), channel_id=2, replica_groups={{0,8,16,24},{4,12,20,28},{1,9,17,25},{5,13,21,29},{2,10,18,26},{6,14,22..., dimensions={0}, use_global_device_ids=true | all-gather | bytes 655360 | tf_op jit(solution)/shard_map/all_gather | solution.py:517
  26.6 0.0 collective-permute-done.1.refs_9_
  26.6 0.0 collective-permute-done.2.refs_10_
  26.6 1.5 %convolve.1 = (bf16[128,256]{1,0:T(8,128)(2,1)S(1)}, bf16[128,256]{1,0:T(8,128)(2,1)S(1)}, bf16[256,1024]{1,0:T(8,128)(2,1)S(1)}, bf16[256,1024]{1,0:T(8,128)(2,1)S(1)}) custom-call(bf16[256,256]{1,0:T(8,128)(2,1)S(1)} %get-tuple-element.31.refs_10_.refs_0_, bf16[4,256,256]{2,1,0:T(8,128)(2,1)S(1)} %bitcast.5, ...), custom_call_target="tpu_custom_call", output_to_operand_aliasing={{2}: (9, {}), {3}: (10, {})} | custom-call | flops 300000000 | bytes 3145728 | tf_op jit(solution)/shard_map/convolve/pallas_call | solution.py:374
  28.1 0.1 collective-permute-start.6
  28.2 0.5 %collective-permute-start.7 = (bf16[256,1024]{1,0:T(8,128)(2,1)S(1)}, bf16[256,1024]{1,0:T(8,128)(2,1)S(1)}, u32[]{:S(2)}, u32[]{:S(2)}) collective-permute-start(bf16[256,1024]{1,0:T(8,128)(2,1)S(1)} %get-tuple-element.44.refs_2_), channel_id=1, source_target_pairs={{0,4},{4,0},{8,12},{12,8},{16,20},{20,16},{24,28},{28,24},{1,5},{5... | collective-permute-start | bytes 1572872 | tf_op jit(solution)/shard_map/ppermute | solution.py:505
  28.7 0.1 collective-permute-start.3
  28.7 2.2 %collective-permute-done.3.theirs_ref = bf16[128,256]{1,0:T(8,128)(2,1)S(1)} collective-permute-done((bf16[128,256]{1,0:T(8,128)(2,1)S(1)}, bf16[128,256]{1,0:T(8,128)(2,1)S(1)}, u32[]{:S(2)}, u32[]{:S(2)}) %collective-permute-start.3) | collective-permute-done | bytes 65568 | tf_op jit(solution)/shard_map/ppermute | solution.py:505
  30.9 0.6 %collective-permute-start.5 = (bf16[128,512]{1,0:T(8,128)(2,1)S(1)}, bf16[128,512]{1,0:T(8,128)(2,1)S(1)}, u32[]{:S(2)}, u32[]{:S(2)}) collective-permute-start(bf16[128,512]{1,0:T(8,128)(2,1)S(1)} %join_channels.1.gated_ref), channel_id=1, source_target_pairs={{0,2},{1,3},{2,0},{3,1},{4,6},{5,7},{6,4},{7,5},{8,10},{9,11},{10,... | collective-permute-start | bytes 393224 | tf_op jit(solution)/shard_map/ppermute | solution.py:502
  31.5 0.5 %collective-permute-start.4 = (bf16[128,512]{1,0:T(8,128)(2,1)S(1)}, bf16[128,512]{1,0:T(8,128)(2,1)S(1)}, u32[]{:S(2)}, u32[]{:S(2)}) collective-permute-start(bf16[128,512]{1,0:T(8,128)(2,1)S(1)} %join_channels.1.gated_ref), channel_id=1, source_target_pairs={{0,1},{1,0},{2,3},{3,2},{4,5},{5,4},{6,7},{7,6},{8,9},{9,8},{10,11... | collective-permute-start | bytes 393224 | tf_op jit(solution)/shard_map/ppermute | solution.py:502
  32.0 2.0 %own_channels.1 = (f32[128,512]{1,0:T(8,128)S(1)}, f32[128,512]{1,0:T(8,128)S(1)}, f32[128,512]{1,0:T(8,128)S(1)}, f32[128,512]{1,0:T(8,128)S(1)}) custom-call(bf16[128,512]{1,0:T(8,128)(2,1)S(1)} %join_channels.1.gated_ref, bf16[512,4096]{1,0:T(8,128)(2,1)} %weight_ref.3), custom_call_target="tpu_custom_call" | custom-call | flops 268435456 | bytes 3145728 | tf_op jit(solution)/shard_map/own_channels/pallas_call | solution.py:470
  34.0 2.5 %collective-permute-done.5.y_ref = bf16[128,512]{1,0:T(8,128)(2,1)S(1)} collective-permute-done((bf16[128,512]{1,0:T(8,128)(2,1)S(1)}, bf16[128,512]{1,0:T(8,128)(2,1)S(1)}, u32[]{:S(2)}, u32[]{:S(2)}) %collective-permute-start.5) | collective-permute-done | bytes 131104 | tf_op jit(solution)/shard_map/ppermute | solution.py:502
  36.5 0.2 collective-permute-done.4.x_ref
  36.7 0.0 collective-permute-done.6.refs_1_
  36.7 0.0 collective-permute-done.7.refs_3_
  36.7 0.3 sums_to_send.1
  37.1 1.6 %collective-permute-start.8 = (bf16[128,512]{1,0:T(8,128)(2,1)S(1)}, bf16[128,512]{1,0:T(8,128)(2,1)S(1)}, u32[]{:S(2)}, u32[]{:S(2)}) collective-permute-start(bf16[128,512]{1,0:T(8,128)(2,1)S(1)} %get-tuple-element.51), channel_id=1, source_target_pairs={{0,2},{1,3},{2,0},{3,1},{4,6},{5,7},{6,4},{7,5},{8,10},{9,11},{10,... | collective-permute-start | bytes 393224 | tf_op jit(solution)/shard_map/ppermute | solution.py:502
  38.7 0.5 %collective-permute-start.9 = (bf16[128,512]{1,0:T(8,128)(2,1)S(1)}, bf16[128,512]{1,0:T(8,128)(2,1)S(1)}, u32[]{:S(2)}, u32[]{:S(2)}) collective-permute-start(bf16[128,512]{1,0:T(8,128)(2,1)S(1)} %get-tuple-element.52), channel_id=1, source_target_pairs={{0,1},{1,0},{2,3},{3,2},{4,5},{5,4},{6,7},{7,6},{8,9},{9,8},{10,11... | collective-permute-start | bytes 393224 | tf_op jit(solution)/shard_map/ppermute | solution.py:502
  39.2 0.3 sums_to_keep.1
  39.5 2.6 %collective-permute-done.8.refs_2_ = bf16[128,512]{1,0:T(8,128)(2,1)S(1)} collective-permute-done((bf16[128,512]{1,0:T(8,128)(2,1)S(1)}, bf16[128,512]{1,0:T(8,128)(2,1)S(1)}, u32[]{:S(2)}, u32[]{:S(2)}) %collective-permute-start.8) | collective-permute-done | bytes 131104 | tf_op jit(solution)/shard_map/ppermute | solution.py:502
  42.1 1.5 %collective-permute-done.9.refs_3_ = bf16[128,512]{1,0:T(8,128)(2,1)S(1)} collective-permute-done((bf16[128,512]{1,0:T(8,128)(2,1)S(1)}, bf16[128,512]{1,0:T(8,128)(2,1)S(1)}, u32[]{:S(2)}, u32[]{:S(2)}) %collective-permute-start.9) | collective-permute-done | bytes 131104 | tf_op jit(solution)/shard_map/ppermute | solution.py:502
  43.6 0.7 %last_sum.1 = bf16[128,1024]{1,0:T(8,128)(2,1)} custom-call(f32[128,512]{1,0:T(8,128)S(1)} %get-tuple-element.47.refs_0_, f32[128,512]{1,0:T(8,128)S(1)} %get-tuple-element.48.refs_1_, bf16[128,512]{1,0:T(8,128)(2,1)S(1)} %collective-permute-done.8.refs_2_, bf16[128,512]{1,0:T(8,128)(2,1)S(1)} %collective-permute-done.9.refs_3_), custom_call_target="tpu_custom_call" | custom-call | flops 1000000 | bytes 1048576 | tf_op jit(solution)/shard_map/last_sum/pallas_call | solution.py:455
  (2 shorter events, 0.1 us)
Async XLA Ops:
  1.4 25.2 %collective-permute-start.1 = (bf16[256,1024]{1,0:T(8,128)(2,1)S(1)}, bf16[256,1024]{1,0:T(8,128)(2,1)S(1)}, u32[]{:S(2)}, u32[]{:S(2)}) collective-permute-start(bf16[256,1024]{1,0:T(8,128)(2,1)S(1)} %get-tuple-element.39), channel_id=1, source_target_pairs={{0,1},{1,0},{2,3},{3,2},{4,5},{5,4},{6,7},{7,6},{8,9},{9,8},{10,11... | collective-permute-start | bytes 1572872 | tf_op jit(solution)/shard_map/ppermute | solution.py:502
  4.4 22.2 %collective-permute-start.2 = (bf16[256,1024]{1,0:T(8,128)(2,1)S(1)}, bf16[256,1024]{1,0:T(8,128)(2,1)S(1)}, u32[]{:S(2)}, u32[]{:S(2)}) collective-permute-start(bf16[256,1024]{1,0:T(8,128)(2,1)S(1)} %get-tuple-element.40), channel_id=1, source_target_pairs={{0,2},{1,3},{2,0},{3,1},{4,6},{5,7},{6,4},{7,5},{8,10},{9,11},{10,... | collective-permute-start | bytes 1572872 | tf_op jit(solution)/shard_map/ppermute | solution.py:502
  5.9 1.3 %collective-permute-start = (bf16[256,256]{1,0:T(8,128)(2,1)S(1)}, bf16[256,256]{1,0:T(8,128)(2,1)S(1)}, u32[]{:S(2)}, u32[]{:S(2)}) collective-permute-start(bf16[256,256]{1,0:T(8,128)(2,1)S(1)} %get-tuple-element.30), channel_id=1, source_target_pairs={{0,4},{4,0},{8,12},{12,8},{16,20},{20,16},{24,28},{28,24},{1,5},{5... | collective-permute-start | bytes 393224 | tf_op jit(solution)/shard_map/ppermute | solution.py:505
  28.1 8.7 %collective-permute-start.6 = (bf16[256,1024]{1,0:T(8,128)(2,1)S(1)}, bf16[256,1024]{1,0:T(8,128)(2,1)S(1)}, u32[]{:S(2)}, u32[]{:S(2)}) collective-permute-start(bf16[256,1024]{1,0:T(8,128)(2,1)S(1)} %get-tuple-element.43.refs_0_), channel_id=1, source_target_pairs={{0,4},{4,0},{8,12},{12,8},{16,20},{20,16},{24,28},{28,24},{1,5},{5... | collective-permute-start | bytes 1572872 | tf_op jit(solution)/shard_map/ppermute | solution.py:505
  28.2 8.6 %collective-permute-start.7 = (bf16[256,1024]{1,0:T(8,128)(2,1)S(1)}, bf16[256,1024]{1,0:T(8,128)(2,1)S(1)}, u32[]{:S(2)}, u32[]{:S(2)}) collective-permute-start(bf16[256,1024]{1,0:T(8,128)(2,1)S(1)} %get-tuple-element.44.refs_2_), channel_id=1, source_target_pairs={{0,4},{4,0},{8,12},{12,8},{16,20},{20,16},{24,28},{28,24},{1,5},{5... | collective-permute-start | bytes 1572872 | tf_op jit(solution)/shard_map/ppermute | solution.py:505
  28.7 2.2 %collective-permute-start.3 = (bf16[128,256]{1,0:T(8,128)(2,1)S(1)}, bf16[128,256]{1,0:T(8,128)(2,1)S(1)}, u32[]{:S(2)}, u32[]{:S(2)}) collective-permute-start(bf16[128,256]{1,0:T(8,128)(2,1)S(1)} %get-tuple-element.42), channel_id=1, source_target_pairs={{0,4},{4,0},{8,12},{12,8},{16,20},{20,16},{24,28},{28,24},{1,5},{5... | collective-permute-start | bytes 196616 | tf_op jit(solution)/shard_map/ppermute | solution.py:505
  30.9 5.6 %collective-permute-start.5 = (bf16[128,512]{1,0:T(8,128)(2,1)S(1)}, bf16[128,512]{1,0:T(8,128)(2,1)S(1)}, u32[]{:S(2)}, u32[]{:S(2)}) collective-permute-start(bf16[128,512]{1,0:T(8,128)(2,1)S(1)} %join_channels.1.gated_ref), channel_id=1, source_target_pairs={{0,2},{1,3},{2,0},{3,1},{4,6},{5,7},{6,4},{7,5},{8,10},{9,11},{10,... | collective-permute-start | bytes 393224 | tf_op jit(solution)/shard_map/ppermute | solution.py:502
  31.5 5.3 %collective-permute-start.4 = (bf16[128,512]{1,0:T(8,128)(2,1)S(1)}, bf16[128,512]{1,0:T(8,128)(2,1)S(1)}, u32[]{:S(2)}, u32[]{:S(2)}) collective-permute-start(bf16[128,512]{1,0:T(8,128)(2,1)S(1)} %join_channels.1.gated_ref), channel_id=1, source_target_pairs={{0,1},{1,0},{2,3},{3,2},{4,5},{5,4},{6,7},{7,6},{8,9},{9,8},{10,11... | collective-permute-start | bytes 393224 | tf_op jit(solution)/shard_map/ppermute | solution.py:502
  37.1 5.0 %collective-permute-start.8 = (bf16[128,512]{1,0:T(8,128)(2,1)S(1)}, bf16[128,512]{1,0:T(8,128)(2,1)S(1)}, u32[]{:S(2)}, u32[]{:S(2)}) collective-permute-start(bf16[128,512]{1,0:T(8,128)(2,1)S(1)} %get-tuple-element.51), channel_id=1, source_target_pairs={{0,2},{1,3},{2,0},{3,1},{4,6},{5,7},{6,4},{7,5},{8,10},{9,11},{10,... | collective-permute-start | bytes 393224 | tf_op jit(solution)/shard_map/ppermute | solution.py:502
  38.7 5.0 %collective-permute-start.9 = (bf16[128,512]{1,0:T(8,128)(2,1)S(1)}, bf16[128,512]{1,0:T(8,128)(2,1)S(1)}, u32[]{:S(2)}, u32[]{:S(2)}) collective-permute-start(bf16[128,512]{1,0:T(8,128)(2,1)S(1)} %get-tuple-element.52), channel_id=1, source_target_pairs={{0,1},{1,0},{2,3},{3,2},{4,5},{5,4},{6,7},{7,6},{8,9},{9,8},{10,11... | collective-permute-start | bytes 393224 | tf_op jit(solution)/shard_map/ppermute | solution.py:502

commit v3 on v0

--- a/solution.py
+++ b/solution.py
@@ -111,9 +111,9 @@
 
 
 def filter_kernel(blocks, block, outs, pad, *refs):
-    hbm, refs = refs[:10], refs[10:]
-    hre_ref, him_ref, hfirst_ref, fwd_ref, inv_ref, skip_ref = refs[:6]
-    refs = refs[6:]
+    hbm, refs = refs[:11], refs[11:]
+    hre_ref, him_ref, hfirst_ref, fwd_ref, inv_ref, skip_ref, gate_ref = refs[:7]
+    refs = refs[7:]
     w1_ref, b1_ref, w2_ref, b2_ref, w3_ref, decay_ref, feat_ref, table_ref, back_ref = refs[:9]
     all_skip_ref, first_ref, sems = refs[9:]
     targets = [
@@ -123,9 +123,11 @@
     copies = [
         pltpu.make_async_copy(hbm[i], targets[i], sems.at[i]) for i in range(len(targets))
     ]
+    group = lax.axis_index("seq") % outs
+    lanes = pl.ds(pl.multiple_of(group * LANES, LANES), LANES)
+    copies.append(pltpu.make_async_copy(hbm[10].at[:, lanes], gate_ref, sems.at[10]))
     for copy in copies:
         copy.start()
-    group = lax.axis_index("seq") % outs
     length = blocks * block
     emb, order = w1_ref.shape
     first_ref[...] = jnp.zeros_like(first_ref)
@@ -147,7 +149,6 @@
         + b1
     )
     hidden = fast_sin(layer(hidden, stacked_diagonal(w2_ref[...])) + b2)
-    lanes = pl.ds(pl.multiple_of(group * LANES, LANES), LANES)
     shaped = layer(hidden, stacked_diagonal(w3_ref[:, lanes]))
 
     decay = decay_ref[:, lanes]
@@ -178,8 +179,8 @@
         him_ref[k] = jnp.where(first_row, 0.0, imag)
         hfirst_ref[k] = jnp.where(first_row, imag, real)[:8]
 
-    copies[8].wait()
-    copies[9].wait()
+    for copy in copies[8:]:
+        copy.wait()
     skip_ref[...] = all_skip_ref[:, lanes]
     high, low = split_value(back_ref[...])
     inv_ref[:, : 2 * block] = high
@@ -187,7 +188,7 @@
     inv_ref[:, 4 * block :] = high
 
 
-def call_filter(weights, skip, blocks, outs, block):
+def call_filter(weights, skip, gate, blocks, outs, block):
     w1, b1, w2, b2, w3, decay = weights
     length = blocks * block
     emb, order = w1.shape
@@ -196,7 +197,7 @@
     feats = filter_feature_table(length, emb, pad)
     hbm = [
         w1, feats, b1[None], w2, b2[None], w3, decay[None], forward.astype(np.float32),
-        inverse.astype(np.float32), skip[None],
+        inverse.astype(np.float32), skip[None], gate,
     ]
     out_shape = [
         VMEM((blocks, block, LANES), F32),
@@ -205,6 +206,7 @@
         VMEM((2 * block, 2 * block), BF16),
         VMEM((block, 6 * block), BF16),
         VMEM((1, LANES), F32),
+        VMEM((block, LANES), BF16),
     ]
     return pl.pallas_call(
         functools.partial(filter_kernel, blocks, block, outs, pad),
@@ -256,7 +258,7 @@
 
 
 def pack_kernel(blocks, outs, x_ref, gate_ref, weight_ref, pieces_ref, *refs):
-    gate_refs, (over_x_ref, over_y_ref, sems) = refs[:outs], refs[outs:]
+    gate_refs, (over_x_ref, over_y_ref, sems) = refs[: outs - 1], refs[outs - 1 :]
     group = lax.axis_index("seq") % outs
     copies = [
         pltpu.make_async_copy(
@@ -264,10 +266,10 @@
         )
         for d in range(blocks)
     ]
-    for k in range(outs):
+    for k in range(1, outs):
         lanes = pl.ds(pl.multiple_of((group ^ k) * LANES, LANES), LANES)
         copies.append(
-            pltpu.make_async_copy(gate_ref.at[:, lanes], gate_refs[k], sems.at[len(copies)])
+            pltpu.make_async_copy(gate_ref.at[:, lanes], gate_refs[k - 1], sems.at[len(copies)])
         )
     copies += weight_copies(weight_ref, over_x_ref, over_y_ref, sems, len(copies))
     for copy in copies:
@@ -280,22 +282,21 @@
     block = x.shape[0]
     send = VMEM((weight.shape[0] // 2, weight.shape[1] // FACE), BF16)
     out_shape = [jax.ShapeDtypeStruct((blocks, block, LANES), BF16)]
-    out_shape += [jax.ShapeDtypeStruct((block, LANES), BF16)] * outs + [send] * 2
+    out_shape += [jax.ShapeDtypeStruct((block, LANES), BF16)] * (outs - 1) + [send] * 2
     return pl.pallas_call(
         functools.partial(pack_kernel, blocks, outs),
         in_specs=[pl.BlockSpec(memory_space=pltpu.HBM)] * 3,
         out_specs=[pl.BlockSpec(memory_space=VMEM)] * len(out_shape),
         out_shape=out_shape,
-        scratch_shapes=[pltpu.SemaphoreType.DMA((blocks + outs + 4,))],
+        scratch_shapes=[pltpu.SemaphoreType.DMA((blocks + outs + 3,))],
         cost_estimate=pl.CostEstimate(flops=0, bytes_accessed=2**21, transcendentals=0),
         name="pack_pieces",
     )(*(pltpu.with_memory_space_constraint(each, pltpu.HBM) for each in (x, gate, weight)))
 
 
 def conv_kernel(blocks, outs, block, xs_ref, *refs):
-    gate_refs, refs = refs[:outs], refs[outs:]
-    hre_ref, him_ref, hfirst_ref, fwd_ref, inv_ref, skip_ref = refs[:6]
-    refs = refs[8:]
+    hre_ref, him_ref, hfirst_ref, fwd_ref, inv_ref, skip_ref, gate_ref = refs[:7]
+    refs = refs[9:]
     out_refs, (wre_ref, wim_ref, yre_ref, yim_ref) = refs[:outs], refs[outs + 2 :]
     me = lax.axis_index("seq")
     half, group = me // outs, me % outs
@@ -346,16 +347,22 @@
         conv = jnp.dot(inv_ref[...], pair, preferred_element_type=F32)
         for i in range(2):
             values = xs_ref[half * outs + (group ^ (k + i))].astype(F32)
-            gate = gate_refs[k + i][...].astype(F32)
             mixed = conv[:, i * LANES : (i + 1) * LANES] + skip * values
-            out_refs[k + i][...] = (gate * mixed).astype(BF16)
-
-
-def call_conv(xs, gates, filters, passing):
+            if k + i == 0:
+                mixed = (gate_ref[...].astype(F32) * mixed).astype(BF16)
+            out_refs[k + i][...] = mixed
+
+
+def gate_kernel(count, *refs):
+    for k in range(count):
+        gate = refs[count + k][...].astype(F32)
+        refs[2 * count + k][...] = (gate * refs[k][...]).astype(BF16)
+
+
+def call_conv(xs, filters, passing, outs):
     blocks, block, _ = xs.shape
-    outs = len(gates)
     pinned = [pltpu.with_memory_space_constraint(each, VMEM) for each in filters]
-    operands = [xs, *gates, *pinned]
+    operands = [xs, *pinned]
     shape = jax.ShapeDtypeStruct
     return pl.pallas_call(
         functools.partial(conv_kernel, blocks, outs, block),
@@ -363,7 +370,8 @@
         + [pl.BlockSpec(memory_space=pl.ANY)] * 2,
         out_specs=[pl.BlockSpec(memory_space=VMEM)] * outs
         + [pl.BlockSpec(memory_space=pl.ANY)] * 2,
-        out_shape=[shape((block, LANES), BF16)] * outs + [shape(p.shape, p.dtype) for p in passing],
+        out_shape=[shape((block, LANES), F32 if k else BF16) for k in range(outs)]
+        + [shape(p.shape, p.dtype) for p in passing],
         input_output_aliases={len(operands) + i: outs + i for i in range(2)},
         scratch_shapes=[
             VMEM((blocks, block, LANES), F32),
@@ -490,7 +498,7 @@
 
     along_seq = lambda part, k: lax.ppermute(part, "seq", [(s, s ^ k) for s in range(blocks)])
     along_chan = lambda part, k: lax.ppermute(part, "chan", [(c, c ^ k) for c in range(FACE)])
-    to_partners = lambda parts: [parts[0]] + [along_seq(parts[k], k) for k in range(1, outs)]
+    shape = jax.ShapeDtypeStruct
 
     xs, *gates, over_x, over_y = call_pack(
         mixer_input, gate_branch, output_weight, blocks, outs
@@ -500,14 +508,22 @@
     filters = call_filter(
         (first_weight, first_bias, second_weight, second_bias, last_weight, decay_rate),
         skip_gain,
+        gate_branch,
         blocks,
         outs,
         block,
     )
-    *pieces, from_x, from_y = call_conv(xs, to_partners(gates), filters, (from_x, from_y))
+    gates = [along_seq(gates[k - 1], k) for k in range(1, outs)]
+    first, *mixed, from_x, from_y = call_conv(xs, filters, (from_x, from_y), outs)
     from_x, from_y = (from_x, along_seq(from_x, 1)), (from_y, along_seq(from_y, 1))
-    pieces = to_partners(pieces)
-    shape = jax.ShapeDtypeStruct
+    pieces = in_vmem(
+        functools.partial(gate_kernel, outs - 1),
+        [*mixed, *gates],
+        [shape((block, LANES), BF16)] * (outs - 1),
+        "apply_gates",
+        10**6,
+    )
+    pieces = [first] + [along_seq(pieces[k - 1], k) for k in range(1, outs)]
     gated = in_vmem(
         functools.partial(join_kernel, outs),
         pieces,

time: 42.4 us -> 46.3 us (1.092)
  waiting for transfers between devices: 14 us -> 19 us
  local copies, waits for them, and re-layouts: 0.76 us -> 0.01 us
    all_to_all x1, waiting for transfers between devices: 2.89 us -> 6.88 us  [split_shards(): xs = lax.all_to_all(xs, 'seq', 0, 0, tiled=True)]
    ppermute x8, waiting for transfers between devices: 4.27 us -> 5.33 us  [split_shards(): lax.ppermute(part, 'seq', [(s, s ^ k) for s in range(blocks)])]
    unnamed x2 -> x6, local copies, waits for them, and re-layouts: 0.76 us -> 0.01 us
    pallas_call x4 -> x5, Pallas kernels: 1.41 us -> 1.43 us  [in_vmem(): pl.pallas_call(kernel, in_specs=[pl.BlockSpec(memory_space=VMEM)] * len(o...]
  transfers between devices with their start and end apart: 15 -> 15, of which waited for: 9 -> 9; matrix products, arithmetic and copies ran while one was open for 0% -> 0% of each run, Pallas kernels for 12% -> 11%
where the time goes in v3:
time: 46.3 us; the launch traced here: 46 us
  waiting for transfers between devices  19 us (41%)
  starting transfers between devices  17 us (37%)
  Pallas kernels  9.93 us (21%)
    ppermute x6, starting transfers between devices, split_shards(): lax.ppermute(part, 'chan', [(c, c ^ k) for c in range(FACE)])  7.75 us
    all_to_all x1, waiting for transfers between devices, split_shards(): xs = lax.all_to_all(xs, 'seq', 0, 0, tiled=True)  6.88 us
    ppermute x6, waiting for transfers between devices, split_shards(): lax.ppermute(part, 'chan', [(c, c ^ k) for c in range(FACE)])  6.79 us
    ppermute x8, waiting for transfers between devices, split_shards(): lax.ppermute(part, 'seq', [(s, s ^ k) for s in range(blocks)])  5.33 us
    all_to_all x1, starting transfers between devices, split_shards(): xs = lax.all_to_all(xs, 'seq', 0, 0, tiled=True)  4.88 us
    ppermute x8, starting transfers between devices, split_shards(): lax.ppermute(part, 'seq', [(s, s ^ k) for s in range(blocks)])  4.37 us
    pallas_call x1, Pallas kernels, call_filter(): pl.pallas_call(functools.partial(filter_kernel, blocks, block, outs, pad)...  2.85 us
    pallas_call x1, Pallas kernels, call_pack(): pl.pallas_call(functools.partial(pack_kernel, blocks, outs), in_specs=[pl...  2.46 us
  transfers between devices with their start and end apart: 15, of which 9 were waited for; matrix products, arithmetic and copies ran while one was open for 0% of the time, Pallas kernels for 11%

profile of v3, /device:TPU:0, one launch (start us, length us, event | category | flops | bytes accessed | tf_op | source)
XLA Modules:
  0.0 46.0 jit_solution(4646244726696739337)
XLA Ops:
  0.0 2.5 %pack_pieces.1 = (bf16[8,128,128]{2,1,0:T(8,128)(2,1)}, bf16[128,128]{1,0:T(8,128)(2,1)}, bf16[128,128]{1,0:T(8,128)(2,1)}, bf16[128,128]{1,0:T(8,128)(2,1)}, bf...) custom-call(bf16[128,512]{1,0:T(8,128)(2,1)} %x_ref.1, bf16[128,512]{1,0:T(8,128)(2,1)} %refs_10_.1, ...), custom_call_target="tpu_custom_call" | custom-call | bytes 2097152 | tf_op jit(solution)/shard_map/pack_pieces/pallas_call | solution.py:286
  2.5 0.0 copy-start.2
  2.5 0.0 copy-start.1
  2.5 0.0 copy-start
  2.5 3.0 %collective-permute-start = (bf16[256,1024]{1,0:T(8,128)(2,1)}, bf16[256,1024]{1,0:T(8,128)(2,1)S(1)}, u32[]{:S(2)}, u32[]{:S(2)}) collective-permute-start(bf16[256,1024]{1,0:T(8,128)(2,1)} %get-tuple-element.43), channel_id=1, source_target_pairs={{0,1},{1,0},{2,3},{3,2},{4,5},{5,4},{6,7},{7,6},{8,9},{9,8},{10,11... | collective-permute-start | bytes 1572872 | tf_op jit(solution)/shard_map/ppermute | solution.py:500
  5.5 1.5 %collective-permute-start.1 = (bf16[256,1024]{1,0:T(8,128)(2,1)S(1)}, bf16[256,1024]{1,0:T(8,128)(2,1)S(1)}, u32[]{:S(2)}, u32[]{:S(2)}) collective-permute-start(bf16[256,1024]{1,0:T(8,128)(2,1)S(1)} %get-tuple-element.44), channel_id=1, source_target_pairs={{0,2},{1,3},{2,0},{3,1},{4,6},{5,7},{6,4},{7,5},{8,10},{9,11},{10,... | collective-permute-start | bytes 1572872 | tf_op jit(solution)/shard_map/ppermute | solution.py:500
  7.0 4.9 %all-to-all-start = ((bf16[8,128,128]{2,1,0:T(8,128)(2,1)}), bf16[8,128,128]{2,1,0:T(8,128)(2,1)S(1)}, u32[]{:S(2)}, u32[]{:S(2)}) async-start(bf16[8,128,128]{2,1,0:T(8,128)(2,1)} %get-tuple-element.35), calls=%async_computation | async-start | bytes 524288 | tf_op jit(solution)/shard_map/all_to_all | solution.py:506
  11.9 2.9 %filter_spectra.1 = (f32[8,128,128]{2,1,0:T(8,128)S(1)}, f32[8,128,128]{2,1,0:T(8,128)S(1)}, f32[8,8,128]{2,1,0:T(8,128)S(1)}, bf16[256,256]{1,0:T(8,128)(2,1)S(...) custom-call(f32[33,64]{1,0:T(8,128)} %refs_0_.1, ...), custom_call_target="tpu_custom_call" | custom-call | flops 400000000 | bytes 8388608 | tf_op jit(solution)/shard_map/filter_spectra/pallas_call | solution.py:211
  14.8 6.9 %all-to-all-done.xs_ref = bf16[8,128,128]{2,1,0:T(8,128)(2,1)S(1)} async-done(((bf16[8,128,128]{2,1,0:T(8,128)(2,1)}), bf16[8,128,128]{2,1,0:T(8,128)(2,1)S(1)}, u32[]{:S(2)}, u32[]{:S(2)}) %all-to-all-start) | async-done | bytes 262176 | tf_op jit(solution)/shard_map/all_to_all | solution.py:506
  21.6 0.0 collective-permute-done.refs_7_
  21.6 0.0 collective-permute-done.1.refs_8_
  21.7 1.2 %convolve.1 = (bf16[128,128]{1,0:T(8,128)(2,1)S(1)}, f32[128,128]{1,0:T(8,128)S(1)}, f32[128,128]{1,0:T(8,128)S(1)}, f32[128,128]{1,0:T(8,128)S(1)}, bf16[256,10...) custom-call(bf16[8,128,128]{2,1,0:T(8,128)(2,1)S(1)} %all-to-all-done.xs_ref, ...), custom_call_target="tpu_custom_call", output_to_operand_aliasing={{4}: (8, {}), {5}: (9, {})} | custom-call | flops 200000000 | bytes 3145728 | tf_op jit(solution)/shard_map/convolve/pallas_call | solution.py:367
  22.8 0.1 collective-permute-start.10
  22.9 0.5 %collective-permute-start.11 = (bf16[256,1024]{1,0:T(8,128)(2,1)S(1)}, bf16[256,1024]{1,0:T(8,128)(2,1)S(1)}, u32[]{:S(2)}, u32[]{:S(2)}) collective-permute-start(bf16[256,1024]{1,0:T(8,128)(2,1)S(1)} %get-tuple-element.56.refs_2_), channel_id=1, source_target_pairs={{0,4},{4,0},{8,12},{12,8},{16,20},{20,16},{24,28},{28,24},{1,5},{5... | collective-permute-start | bytes 1572872 | tf_op jit(solution)/shard_map/ppermute | solution.py:499
  23.4 0.0 copy-done.2
  23.4 0.1 collective-permute-start.2
  23.5 0.0 copy-done.1
  23.5 0.2 collective-permute-start.3
  23.6 0.0 copy-done
  23.7 1.6 %collective-permute-start.4 = (bf16[128,128]{1,0:T(8,128)(2,1)S(1)}, bf16[128,128]{1,0:T(8,128)(2,1)S(1)}, u32[]{:S(2)}, u32[]{:S(2)}) collective-permute-start(bf16[128,128]{1,0:T(8,128)(2,1)S(1)} %copy-done), channel_id=1, source_target_pairs={{0,12},{4,8},{8,4},{12,0},{16,28},{20,24},{24,20},{28,16},{1,13},{... | collective-permute-start | bytes 98312 | tf_op jit(solution)/shard_map/ppermute | solution.py:499
  25.3 0.3 collective-permute-done.2.refs_3_
  25.6 2.0 %collective-permute-done.3.refs_4_ = bf16[128,128]{1,0:T(8,128)(2,1)S(1)} collective-permute-done((bf16[128,128]{1,0:T(8,128)(2,1)S(1)}, bf16[128,128]{1,0:T(8,128)(2,1)S(1)}, u32[]{:S(2)}, u32[]{:S(2)}) %collective-permute-start.3) | collective-permute-done | bytes 32800 | tf_op jit(solution)/shard_map/ppermute | solution.py:499
  27.6 0.0 collective-permute-done.4.refs_5_
  27.6 0.2 collective-permute-start.5
  27.8 1.3 %collective-permute-start.6 = (bf16[128,128]{1,0:T(8,128)(2,1)S(1)}, bf16[128,128]{1,0:T(8,128)(2,1)S(1)}, u32[]{:S(2)}, u32[]{:S(2)}) collective-permute-start(bf16[128,128]{1,0:T(8,128)(2,1)S(1)} %get-tuple-element.53), channel_id=1, source_target_pairs={{0,8},{4,12},{8,0},{12,4},{16,24},{20,28},{24,16},{28,20},{1,9},{5... | collective-permute-start | bytes 98312 | tf_op jit(solution)/shard_map/ppermute | solution.py:499
  29.1 0.4 collective-permute-start.7
  29.5 0.0 collective-permute-done.5.refs_1_
  29.5 2.2 %collective-permute-done.6.refs_2_ = bf16[128,128]{1,0:T(8,128)(2,1)S(1)} collective-permute-done((bf16[128,128]{1,0:T(8,128)(2,1)S(1)}, bf16[128,128]{1,0:T(8,128)(2,1)S(1)}, u32[]{:S(2)}, u32[]{:S(2)}) %collective-permute-start.6) | collective-permute-done | bytes 32800 | tf_op jit(solution)/shard_map/ppermute | solution.py:499
  31.8 0.8 %collective-permute-done.7.refs_3_ = bf16[128,128]{1,0:T(8,128)(2,1)S(1)} collective-permute-done((bf16[128,128]{1,0:T(8,128)(2,1)S(1)}, bf16[128,128]{1,0:T(8,128)(2,1)S(1)}, u32[]{:S(2)}, u32[]{:S(2)}) %collective-permute-start.7) | collective-permute-done | bytes 32800 | tf_op jit(solution)/shard_map/ppermute | solution.py:499
  32.6 0.6 %collective-permute-start.9 = (bf16[128,512]{1,0:T(8,128)(2,1)S(1)}, bf16[128,512]{1,0:T(8,128)(2,1)S(1)}, u32[]{:S(2)}, u32[]{:S(2)}) collective-permute-start(bf16[128,512]{1,0:T(8,128)(2,1)S(1)} %join_pieces.1.gated_ref), channel_id=1, source_target_pairs={{0,2},{1,3},{2,0},{3,1},{4,6},{5,7},{6,4},{7,5},{8,10},{9,11},{10,... | collective-permute-start | bytes 393224 | tf_op jit(solution)/shard_map/ppermute | solution.py:500
  33.2 0.5 %collective-permute-start.8 = (bf16[128,512]{1,0:T(8,128)(2,1)S(1)}, bf16[128,512]{1,0:T(8,128)(2,1)S(1)}, u32[]{:S(2)}, u32[]{:S(2)}) collective-permute-start(bf16[128,512]{1,0:T(8,128)(2,1)S(1)} %join_pieces.1.gated_ref), channel_id=1, source_target_pairs={{0,1},{1,0},{2,3},{3,2},{4,5},{5,4},{6,7},{7,6},{8,9},{9,8},{10,11... | collective-permute-start | bytes 393224 | tf_op jit(solution)/shard_map/ppermute | solution.py:500
  33.7 2.0 %own_channels.1 = (f32[128,512]{1,0:T(8,128)S(1)}, f32[128,512]{1,0:T(8,128)S(1)}, f32[128,512]{1,0:T(8,128)S(1)}, f32[128,512]{1,0:T(8,128)S(1)}) custom-call(bf16[128,512]{1,0:T(8,128)(2,1)S(1)} %join_pieces.1.gated_ref, bf16[512,4096]{1,0:T(8,128)(2,1)} %weight_ref.3), custom_call_target="tpu_custom_call" | custom-call | flops 268435456 | bytes 3145728 | tf_op jit(solution)/shard_map/own_channels/pallas_call | solution.py:466
  35.7 2.4 %collective-permute-done.9.y_ref = bf16[128,512]{1,0:T(8,128)(2,1)S(1)} collective-permute-done((bf16[128,512]{1,0:T(8,128)(2,1)S(1)}, bf16[128,512]{1,0:T(8,128)(2,1)S(1)}, u32[]{:S(2)}, u32[]{:S(2)}) %collective-permute-start.9) | collective-permute-done | bytes 131104 | tf_op jit(solution)/shard_map/ppermute | solution.py:500
  38.2 0.2 collective-permute-done.8.x_ref
  38.4 0.0 collective-permute-done.10.refs_1_
  38.4 0.0 collective-permute-done.11.refs_3_
  38.4 0.3 sums_to_send.1
  38.7 1.6 %collective-permute-start.12 = (bf16[128,512]{1,0:T(8,128)(2,1)S(1)}, bf16[128,512]{1,0:T(8,128)(2,1)S(1)}, u32[]{:S(2)}, u32[]{:S(2)}) collective-permute-start(bf16[128,512]{1,0:T(8,128)(2,1)S(1)} %get-tuple-element.63), channel_id=1, source_target_pairs={{0,2},{1,3},{2,0},{3,1},{4,6},{5,7},{6,4},{7,5},{8,10},{9,11},{10,... | collective-permute-start | bytes 393224 | tf_op jit(solution)/shard_map/ppermute | solution.py:500
  40.3 0.5 %collective-permute-start.13 = (bf16[128,512]{1,0:T(8,128)(2,1)S(1)}, bf16[128,512]{1,0:T(8,128)(2,1)S(1)}, u32[]{:S(2)}, u32[]{:S(2)}) collective-permute-start(bf16[128,512]{1,0:T(8,128)(2,1)S(1)} %get-tuple-element.64), channel_id=1, source_target_pairs={{0,1},{1,0},{2,3},{3,2},{4,5},{5,4},{6,7},{7,6},{8,9},{9,8},{10,11... | collective-permute-start | bytes 393224 | tf_op jit(solution)/shard_map/ppermute | solution.py:500
  40.9 0.3 sums_to_keep.1
  41.2 2.6 %collective-permute-done.12.refs_2_ = bf16[128,512]{1,0:T(8,128)(2,1)S(1)} collective-permute-done((bf16[128,512]{1,0:T(8,128)(2,1)S(1)}, bf16[128,512]{1,0:T(8,128)(2,1)S(1)}, u32[]{:S(2)}, u32[]{:S(2)}) %collective-permute-start.12) | collective-permute-done | bytes 131104 | tf_op jit(solution)/shard_map/ppermute | solution.py:500
  43.8 1.5 %collective-permute-done.13.refs_3_ = bf16[128,512]{1,0:T(8,128)(2,1)S(1)} collective-permute-done((bf16[128,512]{1,0:T(8,128)(2,1)S(1)}, bf16[128,512]{1,0:T(8,128)(2,1)S(1)}, u32[]{:S(2)}, u32[]{:S(2)}) %collective-permute-start.13) | collective-permute-done | bytes 131104 | tf_op jit(solution)/shard_map/ppermute | solution.py:500
  45.3 0.7 %last_sum.1 = bf16[128,1024]{1,0:T(8,128)(2,1)} custom-call(f32[128,512]{1,0:T(8,128)S(1)} %get-tuple-element.59.refs_0_, f32[128,512]{1,0:T(8,128)S(1)} %get-tuple-element.60.refs_1_, bf16[128,512]{1,0:T(8,128)(2,1)S(1)} %collective-permute-done.12.refs_2_, bf16[128,512]{1,0:T(8,128)(2,1)S(1)} %collective-permute-done.13.refs_3_), custom_call_target="tpu_custom_call" | custom-call | flops 1000000 | bytes 1048576 | tf_op jit(solution)/shard_map/last_sum/pallas_call | solution.py:451
  (2 shorter events, 0.1 us)
Async XLA Ops:
  2.5 20.9 %copy-start.2 = (bf16[128,128]{1,0:T(8,128)(2,1)S(1)}, bf16[128,128]{1,0:T(8,128)(2,1)}, u32[]{:S(2)}) copy-start(bf16[128,128]{1,0:T(8,128)(2,1)} %get-tuple-element.49) | copy-start | bytes 98308
  2.5 21.0 %copy-start.1 = (bf16[128,128]{1,0:T(8,128)(2,1)S(1)}, bf16[128,128]{1,0:T(8,128)(2,1)}, u32[]{:S(2)}) copy-start(bf16[128,128]{1,0:T(8,128)(2,1)} %get-tuple-element.50) | copy-start | bytes 98308
  2.5 21.2 %copy-start = (bf16[128,128]{1,0:T(8,128)(2,1)S(1)}, bf16[128,128]{1,0:T(8,128)(2,1)}, u32[]{:S(2)}) copy-start(bf16[128,128]{1,0:T(8,128)(2,1)} %get-tuple-element.51) | copy-start | bytes 98308
  2.5 19.2 %collective-permute-start = (bf16[256,1024]{1,0:T(8,128)(2,1)}, bf16[256,1024]{1,0:T(8,128)(2,1)S(1)}, u32[]{:S(2)}, u32[]{:S(2)}) collective-permute-start(bf16[256,1024]{1,0:T(8,128)(2,1)} %get-tuple-element.43), channel_id=1, source_target_pairs={{0,1},{1,0},{2,3},{3,2},{4,5},{5,4},{6,7},{7,6},{8,9},{9,8},{10,11... | collective-permute-start | bytes 1572872 | tf_op jit(solution)/shard_map/ppermute | solution.py:500
  5.5 16.1 %collective-permute-start.1 = (bf16[256,1024]{1,0:T(8,128)(2,1)S(1)}, bf16[256,1024]{1,0:T(8,128)(2,1)S(1)}, u32[]{:S(2)}, u32[]{:S(2)}) collective-permute-start(bf16[256,1024]{1,0:T(8,128)(2,1)S(1)} %get-tuple-element.44), channel_id=1, source_target_pairs={{0,2},{1,3},{2,0},{3,1},{4,6},{5,7},{6,4},{7,5},{8,10},{9,11},{10,... | collective-permute-start | bytes 1572872 | tf_op jit(solution)/shard_map/ppermute | solution.py:500
  7.0 14.6 %all-to-all-start = ((bf16[8,128,128]{2,1,0:T(8,128)(2,1)}), bf16[8,128,128]{2,1,0:T(8,128)(2,1)S(1)}, u32[]{:S(2)}, u32[]{:S(2)}) async-start(bf16[8,128,128]{2,1,0:T(8,128)(2,1)} %get-tuple-element.35), calls=%async_computation | async-start | bytes 524288 | tf_op jit(solution)/shard_map/all_to_all | solution.py:506
  22.8 15.6 %collective-permute-start.10 = (bf16[256,1024]{1,0:T(8,128)(2,1)S(1)}, bf16[256,1024]{1,0:T(8,128)(2,1)S(1)}, u32[]{:S(2)}, u32[]{:S(2)}) collective-permute-start(bf16[256,1024]{1,0:T(8,128)(2,1)S(1)} %get-tuple-element.55.refs_0_), channel_id=1, source_target_pairs={{0,4},{4,0},{8,12},{12,8},{16,20},{20,16},{24,28},{28,24},{1,5},{5... | collective-permute-start | bytes 1572872 | tf_op jit(solution)/shard_map/ppermute | solution.py:499
  22.9 15.5 %collective-permute-start.11 = (bf16[256,1024]{1,0:T(8,128)(2,1)S(1)}, bf16[256,1024]{1,0:T(8,128)(2,1)S(1)}, u32[]{:S(2)}, u32[]{:S(2)}) collective-permute-start(bf16[256,1024]{1,0:T(8,128)(2,1)S(1)} %get-tuple-element.56.refs_2_), channel_id=1, source_target_pairs={{0,4},{4,0},{8,12},{12,8},{16,20},{20,16},{24,28},{28,24},{1,5},{5... | collective-permute-start | bytes 1572872 | tf_op jit(solution)/shard_map/ppermute | solution.py:499
  23.4 2.2 %collective-permute-start.2 = (bf16[128,128]{1,0:T(8,128)(2,1)S(1)}, bf16[128,128]{1,0:T(8,128)(2,1)S(1)}, u32[]{:S(2)}, u32[]{:S(2)}) collective-permute-start(bf16[128,128]{1,0:T(8,128)(2,1)S(1)} %copy-done.2), channel_id=1, source_target_pairs={{0,4},{4,0},{8,12},{12,8},{16,20},{20,16},{24,28},{28,24},{1,5},{5... | collective-permute-start | bytes 98312 | tf_op jit(solution)/shard_map/ppermute | solution.py:499
  23.5 4.1 %collective-permute-start.3 = (bf16[128,128]{1,0:T(8,128)(2,1)S(1)}, bf16[128,128]{1,0:T(8,128)(2,1)S(1)}, u32[]{:S(2)}, u32[]{:S(2)}) collective-permute-start(bf16[128,128]{1,0:T(8,128)(2,1)S(1)} %copy-done.1), channel_id=1, source_target_pairs={{0,8},{4,12},{8,0},{12,4},{16,24},{20,28},{24,16},{28,20},{1,9},{5... | collective-permute-start | bytes 98312 | tf_op jit(solution)/shard_map/ppermute | solution.py:499
  23.7 3.9 %collective-permute-start.4 = (bf16[128,128]{1,0:T(8,128)(2,1)S(1)}, bf16[128,128]{1,0:T(8,128)(2,1)S(1)}, u32[]{:S(2)}, u32[]{:S(2)}) collective-permute-start(bf16[128,128]{1,0:T(8,128)(2,1)S(1)} %copy-done), channel_id=1, source_target_pairs={{0,12},{4,8},{8,4},{12,0},{16,28},{20,24},{24,20},{28,16},{1,13},{... | collective-permute-start | bytes 98312 | tf_op jit(solution)/shard_map/ppermute | solution.py:499
  27.6 1.9 %collective-permute-start.5 = (bf16[128,128]{1,0:T(8,128)(2,1)S(1)}, bf16[128,128]{1,0:T(8,128)(2,1)S(1)}, u32[]{:S(2)}, u32[]{:S(2)}) collective-permute-start(bf16[128,128]{1,0:T(8,128)(2,1)S(1)} %get-tuple-element.52), channel_id=1, source_target_pairs={{0,4},{4,0},{8,12},{12,8},{16,20},{20,16},{24,28},{28,24},{1,5},{5... | collective-permute-start | bytes 98312 | tf_op jit(solution)/shard_map/ppermute | solution.py:499
  27.8 3.9 %collective-permute-start.6 = (bf16[128,128]{1,0:T(8,128)(2,1)S(1)}, bf16[128,128]{1,0:T(8,128)(2,1)S(1)}, u32[]{:S(2)}, u32[]{:S(2)}) collective-permute-start(bf16[128,128]{1,0:T(8,128)(2,1)S(1)} %get-tuple-element.53), channel_id=1, source_target_pairs={{0,8},{4,12},{8,0},{12,4},{16,24},{20,28},{24,16},{28,20},{1,9},{5... | collective-permute-start | bytes 98312 | tf_op jit(solution)/shard_map/ppermute | solution.py:499
  29.1 3.4 %collective-permute-start.7 = (bf16[128,128]{1,0:T(8,128)(2,1)S(1)}, bf16[128,128]{1,0:T(8,128)(2,1)S(1)}, u32[]{:S(2)}, u32[]{:S(2)}) collective-permute-start(bf16[128,128]{1,0:T(8,128)(2,1)S(1)} %get-tuple-element.54), channel_id=1, source_target_pairs={{0,12},{4,8},{8,4},{12,0},{16,28},{20,24},{24,20},{28,16},{1,13},{... | collective-permute-start | bytes 98312 | tf_op jit(solution)/shard_map/ppermute | solution.py:499
  32.6 5.6 %collective-permute-start.9 = (bf16[128,512]{1,0:T(8,128)(2,1)S(1)}, bf16[128,512]{1,0:T(8,128)(2,1)S(1)}, u32[]{:S(2)}, u32[]{:S(2)}) collective-permute-start(bf16[128,512]{1,0:T(8,128)(2,1)S(1)} %join_pieces.1.gated_ref), channel_id=1, source_target_pairs={{0,2},{1,3},{2,0},{3,1},{4,6},{5,7},{6,4},{7,5},{8,10},{9,11},{10,... | collective-permute-start | bytes 393224 | tf_op jit(solution)/shard_map/ppermute | solution.py:500
  33.2 5.2 %collective-permute-start.8 = (bf16[128,512]{1,0:T(8,128)(2,1)S(1)}, bf16[128,512]{1,0:T(8,128)(2,1)S(1)}, u32[]{:S(2)}, u32[]{:S(2)}) collective-permute-start(bf16[128,512]{1,0:T(8,128)(2,1)S(1)} %join_pieces.1.gated_ref), channel_id=1, source_target_pairs={{0,1},{1,0},{2,3},{3,2},{4,5},{5,4},{6,7},{7,6},{8,9},{9,8},{10,11... | collective-permute-start | bytes 393224 | tf_op jit(solution)/shard_map/ppermute | solution.py:500
  38.7 5.0 %collective-permute-start.12 = (bf16[128,512]{1,0:T(8,128)(2,1)S(1)}, bf16[128,512]{1,0:T(8,128)(2,1)S(1)}, u32[]{:S(2)}, u32[]{:S(2)}) collective-permute-start(bf16[128,512]{1,0:T(8,128)(2,1)S(1)} %get-tuple-element.63), channel_id=1, source_target_pairs={{0,2},{1,3},{2,0},{3,1},{4,6},{5,7},{6,4},{7,5},{8,10},{9,11},{10,... | collective-permute-start | bytes 393224 | tf_op jit(solution)/shard_map/ppermute | solution.py:500
  40.3 5.0 %collective-permute-start.13 = (bf16[128,512]{1,0:T(8,128)(2,1)S(1)}, bf16[128,512]{1,0:T(8,128)(2,1)S(1)}, u32[]{:S(2)}, u32[]{:S(2)}) collective-permute-start(bf16[128,512]{1,0:T(8,128)(2,1)S(1)} %get-tuple-element.64), channel_id=1, source_target_pairs={{0,1},{1,0},{2,3},{3,2},{4,5},{5,4},{6,7},{7,6},{8,9},{9,8},{10,11... | collective-permute-start | bytes 393224 | tf_op jit(solution)/shard_map/ppermute | solution.py:500
